TPU v7x, 32 devices: a whole 2x2x4 slice. The times are simulated.
32 devices in a mesh: section: 4 (over y, x), tile: 8 (over z, core).
Axes of the slice: x: 2, y: 2, z: 4, core: 2. Of those that a mesh axis runs over, the one named last changes fastest.
Arguments:
- inputs: bfloat16 [4, 8, 16, 1024], P(None, 'tile'), may hold values from -40 to 40
- cotangent: bfloat16 [4, 8, 16, 1024], P(None, 'tile'), may hold values from -6 to 6
- depth_weight: bfloat16 [8, 49, 64], P('section'), may hold values from -0.875 to 0.875
- in_weight: bfloat16 [8, 64, 256], P('section'), may hold values from -0.75 to 0.75
- out_weight: bfloat16 [8, 256, 64], P('section'), may hold values from -0.375 to 0.375
- neighbours: int32 [8, 8], P('tile'), may hold values from -1 to 7, as said below
- orientation: int32 [8], replicated, may hold values from 0 to 3, as said below
Outputs:
- section_outputs: bfloat16 [4, 4, 8, 16, 1024], P('section', None, 'tile')
- section_grads: bfloat16 [4, 4, 8, 16, 1024], P('section', None, 'tile')
- depth_grads: float32 [8, 49, 64], P('section')
- in_grads: float32 [8, 64, 256], P('section')
- out_grads: float32 [8, 256, 64], P('section')
Inputs may be any that keep to these rules, and one draw needn't show every extreme that they name: Tile t stores its pixels turned by orientation[t] quarter turns counterclockwise. The tiles form a grid of 4 columns numbered row by row, the numbering closing on itself modulo 8. For local direction k (0 to 3: north, east, south, west; 4 to 7: north-east, south-east, south-west, north-west) the true direction is j = 4 * (k // 4) + (k + orientation[t]) mod 4, and neighbours[t, k] = (t + d_j) mod 8 with d_j = -4, 1, 4, -1, 1 - 4, 5, 3, -4 - 1 for j = 0..7, except that a corner entry is -1 where no tile meets that vertex; if tile t's true north-east corner is -1, so is the true south-west corner of tile (t - 3) mod 8, and no other corner is -1. `orientation`: tile t lies on base face t * 12 // 8; all tiles of one face share one code.
All inputs are finite; a program needn't handle non-finite values.
Results may differ from a plain program's by a relative error of at most 0.022.
Values may be sent and summed in bfloat16 or wider, within the bound.
A program may use at most 64 MiB of HBM per device.

v0:
```python
import math

import jax
import jax.numpy as jnp
from jax import lax
from jax.sharding import PartitionSpec as P

norm_eps = 1e-06
rim_width = 3
kernel_side = 7


def for_sending(shard):

    def short(part):
        return part.astype(jnp.bfloat16) if part.dtype == jnp.float32 else part

    return jax.tree.map(short, shard)


def from_behind(value, axis, steps):
    count = lax.axis_size(axis)
    pairs = [(source, (source + steps) % count) for source in range(count)]
    return lax.ppermute(value, axis, pairs)


def shifted(shard, axis, by):
    length = lax.axis_size(axis)
    pairs = [(i, i + by) for i in range(length) if 0 <= i + by < length]
    return lax.ppermute(shard, axis, pairs)


def layer_norm(values):
    centred = values - jnp.mean(values, axis=-1, keepdims=True)
    spread = jnp.mean(centred * centred, axis=-1, keepdims=True)
    return centred * lax.rsqrt(spread + norm_eps)


def smooth_gate(values):
    return jax.nn.gelu(values, approximate=True)


def depthwise(padded, depth_taps):
    extent = padded.shape[1] - 2 * rim_width
    channels = padded.shape[2]

    def row_step(tap_row, accum_total):
        band = lax.dynamic_slice_in_dim(padded, tap_row, extent, 0).astype(jnp.float32)
        row_taps = lax.dynamic_slice_in_dim(
            depth_taps, tap_row * kernel_side, kernel_side, 0
        ).astype(jnp.float32)
        for tap_col in range(kernel_side):
            accum_total = accum_total + band[:, tap_col : tap_col + extent, :] * row_taps[tap_col]
        return accum_total

    return lax.fori_loop(
        0, kernel_side, row_step, jnp.zeros((extent, extent, channels), jnp.float32)
    )


def depthwise_back(padded, depth_taps, grad_hidden):
    extent = grad_hidden.shape[1]
    side = padded.shape[1]
    channels = padded.shape[2]

    def row_step(tap_row, carry):
        grad_pad, tap_sums = carry
        band = lax.dynamic_slice_in_dim(padded, tap_row, extent, 0).astype(jnp.float32)
        row_taps = lax.dynamic_slice_in_dim(
            depth_taps, tap_row * kernel_side, kernel_side, 0
        ).astype(jnp.float32)
        spread_rows = jnp.zeros((extent, side, channels), jnp.float32)
        row_list = []
        for tap_col in range(kernel_side):
            row_list.append(
                jnp.sum(grad_hidden * band[:, tap_col : tap_col + extent, :], axis=(0, 1))
            )
            spread_rows = spread_rows.at[:, tap_col : tap_col + extent, :].add(
                grad_hidden * row_taps[tap_col]
            )
        previous = lax.dynamic_slice_in_dim(grad_pad, tap_row, extent, 0)
        grad_pad = lax.dynamic_update_slice_in_dim(grad_pad, previous + spread_rows, tap_row, 0)
        tap_sums = lax.dynamic_update_slice_in_dim(
            tap_sums, jnp.stack(row_list), tap_row * kernel_side, 0
        )
        return (grad_pad, tap_sums)

    start = (
        jnp.zeros((side, side, channels), jnp.float32),
        jnp.zeros((kernel_side * kernel_side, channels), jnp.float32),
    )
    grad_pad, tap_sums = lax.fori_loop(0, kernel_side, row_step, start)
    return (tap_sums, grad_pad)


def block_forward(padded, depth_taps, weight_in, weight_out):
    channels = padded.shape[-1]
    hidden = depthwise(padded, depth_taps)
    normed = layer_norm(hidden).astype(jnp.bfloat16)
    flat_rows = normed.reshape(-1, channels)
    gated = smooth_gate(jnp.dot(flat_rows, weight_in, preferred_element_type=jnp.float32)).astype(
        jnp.bfloat16
    )
    branch = jnp.dot(gated, weight_out, preferred_element_type=jnp.float32).reshape(hidden.shape)
    centre = padded[rim_width:-rim_width, rim_width:-rim_width, :].astype(jnp.float32)
    return (centre + branch).astype(jnp.bfloat16)


def block_backward(padded, depth_taps, weight_in, weight_out, upstream):
    channels = padded.shape[-1]
    hidden = depthwise(padded, depth_taps)
    normed = layer_norm(hidden).astype(jnp.bfloat16)
    flat_rows = normed.reshape(-1, channels)
    before = jnp.dot(flat_rows, weight_in, preferred_element_type=jnp.float32)
    gated = smooth_gate(before).astype(jnp.bfloat16)
    flow_rows = upstream.reshape(-1, channels)
    grad_out = jnp.dot(gated.T, flow_rows, preferred_element_type=jnp.float32)
    grad_gated = jnp.dot(flow_rows, weight_out.T, preferred_element_type=jnp.float32)
    grad_before = jax.vjp(smooth_gate, before)[1](grad_gated)[0].astype(jnp.bfloat16)
    grad_in = jnp.dot(flat_rows.T, grad_before, preferred_element_type=jnp.float32)
    grad_normed = jnp.dot(grad_before, weight_in.T, preferred_element_type=jnp.float32).reshape(
        hidden.shape
    )
    grad_hidden = jax.vjp(layer_norm, hidden)[1](grad_normed)[0]
    grad_depth, grad_pad = depthwise_back(padded, depth_taps, grad_hidden)
    return (grad_depth, grad_in, grad_out, grad_pad)


def offers(square):
    turned = [jnp.rot90(square, quarter, axes=(0, 1)) for quarter in range(4)]
    strips = jnp.stack([rotated[-rim_width:, :, :] for rotated in turned], axis=0)
    corners = jnp.stack([rotated[-rim_width:, :rim_width, :] for rotated in turned], axis=0)
    return (strips, corners)


def assemble(square, rim_list):
    north, east, south, west, north_east, south_east, south_west, north_west = rim_list
    top_band = jnp.concatenate([north_west, north, north_east], axis=1)
    middle_band = jnp.concatenate([west, square, east], axis=1)
    bottom_band = jnp.concatenate([south_west, south, south_east], axis=1)
    return jnp.concatenate([top_band, middle_band, bottom_band], axis=0)


def rim_parts(grad_pad):
    extent = grad_pad.shape[1] - 2 * rim_width
    edge_end = extent + rim_width
    return [
        grad_pad[:rim_width, rim_width:edge_end, :],
        grad_pad[rim_width:edge_end, edge_end:, :],
        grad_pad[edge_end:, rim_width:edge_end, :],
        grad_pad[rim_width:edge_end, :rim_width, :],
        grad_pad[:rim_width, edge_end:, :],
        grad_pad[edge_end:, edge_end:, :],
        grad_pad[edge_end:, :rim_width, :],
        grad_pad[:rim_width, :rim_width, :],
    ]


def grid_offsets(tile_count):
    columns = max(tile_count // 8, 4)
    return [-columns, 1, columns, -1, 1 - columns, columns + 1, columns - 1, -columns - 1]


def gather_rims(square, own_code, neighbour_rows, orientation, offsets):
    extent, channels = (square.shape[1], square.shape[2])
    strips, corners = offers(square)
    flat_strips = strips.reshape(4, -1)
    flat_corners = corners.reshape(4, -1)
    arrived = []
    for true_dir in range(8):
        source = flat_strips if true_dir < 4 else flat_corners
        arrived.append(
            from_behind(for_sending(source), "tile", -offsets[true_dir]).astype(source.dtype)
        )
    rim_list = []
    for direction in range(8):
        turn_count = direction % 4
        grouped = jnp.stack(arrived[:4] if direction < 4 else arrived[4:])
        true_mod = (turn_count + own_code) % 4
        chosen = lax.dynamic_index_in_dim(grouped, true_mod, 0, keepdims=False)
        target = neighbour_rows[0, direction]
        quarter = (true_mod - orientation[jnp.maximum(target, 0)]) % 4
        chosen = lax.dynamic_index_in_dim(chosen, quarter, 0, keepdims=False)
        band_width = extent if direction < 4 else rim_width
        segment = jnp.rot90(
            chosen.reshape(rim_width, band_width, channels), -turn_count, axes=(0, 1)
        )
        rim_list.append(jnp.where(target >= 0, segment, jnp.zeros_like(segment)))
    return assemble(square, rim_list)


def return_rims(grad_pad, own_code, neighbour_rows, offsets):
    extent = grad_pad.shape[1] - 2 * rim_width
    channels = grad_pad.shape[2]
    pieces = rim_parts(grad_pad)
    canonical = []
    for direction in range(8):
        segment = jnp.rot90(pieces[direction], direction % 4, axes=(0, 1))
        keep_mask = neighbour_rows[0, direction] >= 0
        canonical.append(jnp.where(keep_mask, segment, jnp.zeros_like(segment)).reshape(-1))
    edge_set = jnp.stack(canonical[:4])
    corner_set = jnp.stack(canonical[4:])
    gathered = jnp.zeros((4, extent, extent, channels), jnp.float32)
    for true_dir in range(8):
        turn_count = (true_dir % 4 - own_code) % 4
        source = edge_set if true_dir < 4 else corner_set
        segment = lax.dynamic_index_in_dim(source, turn_count, 0, keepdims=False)
        received = from_behind(segment, "tile", offsets[true_dir])
        canvas = jnp.zeros((extent, extent, channels), jnp.float32)
        if true_dir < 4:
            canvas = canvas.at[extent - rim_width :, :, :].set(
                received.reshape(rim_width, extent, channels)
            )
        else:
            canvas = canvas.at[extent - rim_width :, :rim_width, :].set(
                received.reshape(rim_width, rim_width, channels)
            )
        selector = (jnp.arange(4) == turn_count).astype(jnp.float32)
        gathered = gathered + selector[:, None, None, None] * canvas[None]
    accum_total = jnp.zeros((extent, extent, channels), jnp.float32)
    for turns_back in range(4):
        accum_total = accum_total + jnp.rot90(gathered[turns_back], -turns_back, axes=(0, 1))
    return accum_total


def on_device(inputs, cotangent, depth_weight, in_weight, out_weight, neighbours, orientation):
    micro_count = inputs.shape[0]
    extent = inputs.shape[2]
    merged = inputs.shape[3]
    channels = depth_weight.shape[2]
    blocks = depth_weight.shape[0]
    tile_count = lax.axis_size("tile")
    section_count = lax.axis_size("section")
    section_id = lax.axis_index("section")
    own_code = orientation[lax.axis_index("tile")]
    offsets = grid_offsets(tile_count)
    grad_scale = 1.0 / math.sqrt(micro_count * tile_count * extent * extent)
    fresh_in = inputs[:, 0]
    fresh_back = cotangent[:, 0]
    padded_side = extent + 2 * rim_width

    def forward_block(square, depth_taps, weight_in, weight_out):
        padded = gather_rims(square, own_code, neighbours, orientation, offsets)
        return (padded, block_forward(padded, depth_taps, weight_in, weight_out))

    def backward_block(padded, upstream, depth_taps, weight_in, weight_out):
        grad_depth, grad_in, grad_out, grad_pad = block_backward(
            padded, depth_taps, weight_in, weight_out, upstream
        )
        returned = return_rims(grad_pad, own_code, neighbours, offsets)
        interior = grad_pad[rim_width:-rim_width, rim_width:-rim_width, :]
        result = (upstream.astype(jnp.float32) + interior + returned).astype(jnp.bfloat16)
        return (result, grad_depth, grad_in, grad_out)

    step_count = micro_count + section_count - 1

    def forward_step(step_id, carry):
        stored, outputs, arriving = carry
        position = step_id - section_id
        active = (position >= 0) & (position < micro_count)
        slot_id = jnp.clip(position, 0, micro_count - 1)
        begin_field = lax.dynamic_index_in_dim(fresh_in, slot_id, 0, keepdims=False)
        square = jnp.where(section_id == 0, begin_field, arriving).reshape(extent, extent, channels)

        def forward_block_step(block_id, inner):
            square, stored = inner
            padded, square = forward_block(
                square, depth_weight[block_id], in_weight[block_id], out_weight[block_id]
            )
            previous = stored[slot_id, block_id]
            stored = stored.at[slot_id, block_id].set(jnp.where(active, padded, previous))
            return (square, stored)

        square, stored = lax.fori_loop(0, blocks, forward_block_step, (square, stored))
        flat_out = square.reshape(extent, merged)
        outputs = outputs.at[slot_id].set(jnp.where(active, flat_out, outputs[slot_id]))
        arriving = shifted(flat_out, "section", 1)
        return (stored, outputs, arriving)

    stored = jnp.zeros((micro_count, blocks, padded_side, padded_side, channels), jnp.bfloat16)
    outputs = jnp.zeros((micro_count, extent, merged), jnp.bfloat16)
    arriving = jnp.zeros((extent, merged), jnp.bfloat16)
    stored, outputs, arriving = lax.fori_loop(
        0, step_count, forward_step, (stored, outputs, arriving)
    )

    def backward_step(step_id, carry):
        sum_depth, sum_in, sum_out, grads_back, arriving = carry
        position = step_id - (section_count - 1 - section_id)
        active = (position >= 0) & (position < micro_count)
        slot_id = jnp.clip(position, 0, micro_count - 1)
        begin_grad = lax.dynamic_index_in_dim(fresh_back, slot_id, 0, keepdims=False)
        upstream = jnp.where(section_id == section_count - 1, begin_grad, arriving).reshape(
            extent, extent, channels
        )

        def backward_block_step(counter, inner):
            upstream, sum_depth, sum_in, sum_out = inner
            block_id = blocks - 1 - counter
            upstream, grad_depth, grad_in, grad_out = backward_block(
                stored[slot_id, block_id],
                upstream,
                depth_weight[block_id],
                in_weight[block_id],
                out_weight[block_id],
            )
            sum_depth = sum_depth.at[block_id].add(jnp.where(active, grad_depth, 0.0))
            sum_in = sum_in.at[block_id].add(jnp.where(active, grad_in, 0.0))
            sum_out = sum_out.at[block_id].add(jnp.where(active, grad_out, 0.0))
            return (upstream, sum_depth, sum_in, sum_out)

        upstream, sum_depth, sum_in, sum_out = lax.fori_loop(
            0, blocks, backward_block_step, (upstream, sum_depth, sum_in, sum_out)
        )
        flat_grad = upstream.reshape(extent, merged)
        grads_back = grads_back.at[slot_id].set(jnp.where(active, flat_grad, grads_back[slot_id]))
        arriving = shifted(flat_grad, "section", -1)
        return (sum_depth, sum_in, sum_out, grads_back, arriving)

    start = (
        jnp.zeros(depth_weight.shape, jnp.float32),
        jnp.zeros(in_weight.shape, jnp.float32),
        jnp.zeros(out_weight.shape, jnp.float32),
        jnp.zeros((micro_count, extent, merged), jnp.bfloat16),
        jnp.zeros((extent, merged), jnp.bfloat16),
    )
    sum_depth, sum_in, sum_out, grads_back, arriving = lax.fori_loop(
        0, step_count, backward_step, start
    )
    local_sums = (sum_depth, sum_in, sum_out)
    section_outputs = outputs[None, :, None]
    section_grads = grads_back[None, :, None]
    depth_sum, in_sum, out_sum = lax.psum((local_sums[0], local_sums[1], local_sums[2]), "tile")
    return (
        section_outputs,
        section_grads,
        depth_sum * grad_scale,
        in_sum * grad_scale,
        out_sum * grad_scale,
    )


def solution(mesh):
    in_specs = (
        P(None, "tile", None, None),
        P(None, "tile", None, None),
        P("section", None, None),
        P("section", None, None),
        P("section", None, None),
        P("tile", None),
        P(),
    )
    out_specs = (
        P("section", None, "tile", None, None),
        P("section", None, "tile", None, None),
        P("section", None, None),
        P("section", None, None),
        P("section", None, None),
    )
    return jax.shard_map(
        on_device, mesh=mesh, in_specs=in_specs, out_specs=out_specs, check_vma=False
    )
```

profile of v0, /device:TPU:0, one launch (start us, length us, event | category | flops | bytes accessed | tf_op | source)
XLA Modules:
  0.0 888.4 jit_solution(12406736147599466914)
XLA Ops:
  33.1 247.5 %while.258 = (s32[]{:T(128)}, bf16[4,2,22,22,64]{4,3,2,1,0:T(8,128)(2,1)S(1)}, bf16[4,16,1024]{2,1,0:T(8,128)(2,1)S(1)}, bf16[16,1024]{1,0:T(8,128)(2,1)S(1)}, p...) while((s32[]{:T(128)}, ...), condition=%wide.region_9.10_spmd, body=%wide.region_0.9_spmd.sunk | while | flops 19146740 | bytes 3706731 | solution.py:283
  34.0 31.0 %while.261 = (s32[]{:T(128)}, bf16[16,16,64]{2,1,0:T(8,128)(2,1)S(1)}, bf16[4,2,22,22,64]{4,3,2,1,0:T(8,128)(2,1)S(1)}, pred[]{:T(512)}, s32[]{:T(128)}, /*index...) while((s32[]{:T(128)}, ...), condition=%wide.region_7.7_spmd, body=%wide.region_1.6_spmd.sunk | while | flops 19097564 | bytes 3181605 | solution.py:274
  71.6 27.5 %while.261 = (s32[]{:T(128)}, bf16[16,16,64]{2,1,0:T(8,128)(2,1)S(1)}, bf16[4,2,22,22,64]{4,3,2,1,0:T(8,128)(2,1)S(1)}, pred[]{:T(512)}, s32[]{:T(128)}, /*index...) while((s32[]{:T(128)}, ...), condition=%wide.region_7.7_spmd, body=%wide.region_1.6_spmd.sunk | while | flops 19097564 | bytes 3181605 | solution.py:274
  105.9 27.4 %while.261 = (s32[]{:T(128)}, bf16[16,16,64]{2,1,0:T(8,128)(2,1)S(1)}, bf16[4,2,22,22,64]{4,3,2,1,0:T(8,128)(2,1)S(1)}, pred[]{:T(512)}, s32[]{:T(128)}, /*index...) while((s32[]{:T(128)}, ...), condition=%wide.region_7.7_spmd, body=%wide.region_1.6_spmd.sunk | while | flops 19097564 | bytes 3181605 | solution.py:274
  140.8 27.4 %while.261 = (s32[]{:T(128)}, bf16[16,16,64]{2,1,0:T(8,128)(2,1)S(1)}, bf16[4,2,22,22,64]{4,3,2,1,0:T(8,128)(2,1)S(1)}, pred[]{:T(512)}, s32[]{:T(128)}, /*index...) while((s32[]{:T(128)}, ...), condition=%wide.region_7.7_spmd, body=%wide.region_1.6_spmd.sunk | while | flops 19097564 | bytes 3181605 | solution.py:274
  176.0 27.5 %while.261 = (s32[]{:T(128)}, bf16[16,16,64]{2,1,0:T(8,128)(2,1)S(1)}, bf16[4,2,22,22,64]{4,3,2,1,0:T(8,128)(2,1)S(1)}, pred[]{:T(512)}, s32[]{:T(128)}, /*index...) while((s32[]{:T(128)}, ...), condition=%wide.region_7.7_spmd, body=%wide.region_1.6_spmd.sunk | while | flops 19097564 | bytes 3181605 | solution.py:274
  211.2 27.5 %while.261 = (s32[]{:T(128)}, bf16[16,16,64]{2,1,0:T(8,128)(2,1)S(1)}, bf16[4,2,22,22,64]{4,3,2,1,0:T(8,128)(2,1)S(1)}, pred[]{:T(512)}, s32[]{:T(128)}, /*index...) while((s32[]{:T(128)}, ...), condition=%wide.region_7.7_spmd, body=%wide.region_1.6_spmd.sunk | while | flops 19097564 | bytes 3181605 | solution.py:274
  246.3 27.4 %while.261 = (s32[]{:T(128)}, bf16[16,16,64]{2,1,0:T(8,128)(2,1)S(1)}, bf16[4,2,22,22,64]{4,3,2,1,0:T(8,128)(2,1)S(1)}, pred[]{:T(512)}, s32[]{:T(128)}, /*index...) while((s32[]{:T(128)}, ...), condition=%wide.region_7.7_spmd, body=%wide.region_1.6_spmd.sunk | while | flops 19097564 | bytes 3181605 | solution.py:274
  281.2 541.2 %while.260 = (s32[]{:T(128)}, f32[2,49,64]{2,1,0:T(8,128)S(1)}, f32[2,64,256]{2,1,0:T(8,128)S(1)}, f32[2,256,64]{1,2,0:T(8,128)S(1)}, bf16[4,16,1024]{2,1,0:T(8,...) while((s32[]{:T(128)}, f32[2,49,64]{2,1,0:T(8,128)S(1)}, ...), condition=%wide.region_30.31_spmd, body=%wide.region_10.30_spmd.sunk | while | flops 46275036 | bytes 11643992 | solution.py:327
  282.1 69.6 %while.262 = (s32[]{:T(128)}, bf16[16,16,64]{2,1,0:T(8,128)(2,1)S(1)}, f32[2,49,64]{2,1,0:T(8,128)S(1)}, f32[2,64,256]{2,1,0:T(8,128)S(1)}, f32[2,256,64]{1,2,0:...) while((s32[]{:T(128)}, ...), condition=%wide.region_28.28_spmd, body=%wide.region_11.27_spmd.sunk | while | flops 46225860 | bytes 11118722 | solution.py:312
  285.6 14.1 %while.264 = (s32[]{:T(128)}, f32[22,22,64]{2,1,0:T(8,128)S(1)}, f32[49,64]{1,0:T(8,128)S(1)}, bf16[49,64]{1,0:T(8,128)(2,1)S(1)}, f32[16,16,64]{2,1,0:T(8,128)S...) while((s32[]{:T(128)}, f32[22,22,64]{2,1,0:T(8,128)S(1)}, ...), condition=%wide.region_26.25_spmd, body=%wide.region_18.24_spmd.sunk | while | flops 487430 | bytes 3453815 | solution.py:92
  320.4 14.1 %while.264 = (s32[]{:T(128)}, f32[22,22,64]{2,1,0:T(8,128)S(1)}, f32[49,64]{1,0:T(8,128)S(1)}, bf16[49,64]{1,0:T(8,128)(2,1)S(1)}, f32[16,16,64]{2,1,0:T(8,128)S...) while((s32[]{:T(128)}, f32[22,22,64]{2,1,0:T(8,128)S(1)}, ...), condition=%wide.region_26.25_spmd, body=%wide.region_18.24_spmd.sunk | while | flops 487430 | bytes 3453815 | solution.py:92
  359.1 69.5 %while.262 = (s32[]{:T(128)}, bf16[16,16,64]{2,1,0:T(8,128)(2,1)S(1)}, f32[2,49,64]{2,1,0:T(8,128)S(1)}, f32[2,64,256]{2,1,0:T(8,128)S(1)}, f32[2,256,64]{1,2,0:...) while((s32[]{:T(128)}, ...), condition=%wide.region_28.28_spmd, body=%wide.region_11.27_spmd.sunk | while | flops 46225860 | bytes 11118722 | solution.py:312
  362.6 14.1 %while.264 = (s32[]{:T(128)}, f32[22,22,64]{2,1,0:T(8,128)S(1)}, f32[49,64]{1,0:T(8,128)S(1)}, bf16[49,64]{1,0:T(8,128)(2,1)S(1)}, f32[16,16,64]{2,1,0:T(8,128)S...) while((s32[]{:T(128)}, f32[22,22,64]{2,1,0:T(8,128)S(1)}, ...), condition=%wide.region_26.25_spmd, body=%wide.region_18.24_spmd.sunk | while | flops 487430 | bytes 3453815 | solution.py:92
  397.5 14.1 %while.264 = (s32[]{:T(128)}, f32[22,22,64]{2,1,0:T(8,128)S(1)}, f32[49,64]{1,0:T(8,128)S(1)}, bf16[49,64]{1,0:T(8,128)(2,1)S(1)}, f32[16,16,64]{2,1,0:T(8,128)S...) while((s32[]{:T(128)}, f32[22,22,64]{2,1,0:T(8,128)S(1)}, ...), condition=%wide.region_26.25_spmd, body=%wide.region_18.24_spmd.sunk | while | flops 487430 | bytes 3453815 | solution.py:92
  436.5 69.6 %while.262 = (s32[]{:T(128)}, bf16[16,16,64]{2,1,0:T(8,128)(2,1)S(1)}, f32[2,49,64]{2,1,0:T(8,128)S(1)}, f32[2,64,256]{2,1,0:T(8,128)S(1)}, f32[2,256,64]{1,2,0:...) while((s32[]{:T(128)}, ...), condition=%wide.region_28.28_spmd, body=%wide.region_11.27_spmd.sunk | while | flops 46225860 | bytes 11118722 | solution.py:312
  439.9 14.1 %while.264 = (s32[]{:T(128)}, f32[22,22,64]{2,1,0:T(8,128)S(1)}, f32[49,64]{1,0:T(8,128)S(1)}, bf16[49,64]{1,0:T(8,128)(2,1)S(1)}, f32[16,16,64]{2,1,0:T(8,128)S...) while((s32[]{:T(128)}, f32[22,22,64]{2,1,0:T(8,128)S(1)}, ...), condition=%wide.region_26.25_spmd, body=%wide.region_18.24_spmd.sunk | while | flops 487430 | bytes 3453815 | solution.py:92
  475.0 14.1 %while.264 = (s32[]{:T(128)}, f32[22,22,64]{2,1,0:T(8,128)S(1)}, f32[49,64]{1,0:T(8,128)S(1)}, bf16[49,64]{1,0:T(8,128)(2,1)S(1)}, f32[16,16,64]{2,1,0:T(8,128)S...) while((s32[]{:T(128)}, f32[22,22,64]{2,1,0:T(8,128)S(1)}, ...), condition=%wide.region_26.25_spmd, body=%wide.region_18.24_spmd.sunk | while | flops 487430 | bytes 3453815 | solution.py:92
  513.8 69.6 %while.262 = (s32[]{:T(128)}, bf16[16,16,64]{2,1,0:T(8,128)(2,1)S(1)}, f32[2,49,64]{2,1,0:T(8,128)S(1)}, f32[2,64,256]{2,1,0:T(8,128)S(1)}, f32[2,256,64]{1,2,0:...) while((s32[]{:T(128)}, ...), condition=%wide.region_28.28_spmd, body=%wide.region_11.27_spmd.sunk | while | flops 46225860 | bytes 11118722 | solution.py:312
  517.3 14.1 %while.264 = (s32[]{:T(128)}, f32[22,22,64]{2,1,0:T(8,128)S(1)}, f32[49,64]{1,0:T(8,128)S(1)}, bf16[49,64]{1,0:T(8,128)(2,1)S(1)}, f32[16,16,64]{2,1,0:T(8,128)S...) while((s32[]{:T(128)}, f32[22,22,64]{2,1,0:T(8,128)S(1)}, ...), condition=%wide.region_26.25_spmd, body=%wide.region_18.24_spmd.sunk | while | flops 487430 | bytes 3453815 | solution.py:92
  552.4 14.1 %while.264 = (s32[]{:T(128)}, f32[22,22,64]{2,1,0:T(8,128)S(1)}, f32[49,64]{1,0:T(8,128)S(1)}, bf16[49,64]{1,0:T(8,128)(2,1)S(1)}, f32[16,16,64]{2,1,0:T(8,128)S...) while((s32[]{:T(128)}, f32[22,22,64]{2,1,0:T(8,128)S(1)}, ...), condition=%wide.region_26.25_spmd, body=%wide.region_18.24_spmd.sunk | while | flops 487430 | bytes 3453815 | solution.py:92
  591.1 69.7 %while.262 = (s32[]{:T(128)}, bf16[16,16,64]{2,1,0:T(8,128)(2,1)S(1)}, f32[2,49,64]{2,1,0:T(8,128)S(1)}, f32[2,64,256]{2,1,0:T(8,128)S(1)}, f32[2,256,64]{1,2,0:...) while((s32[]{:T(128)}, ...), condition=%wide.region_28.28_spmd, body=%wide.region_11.27_spmd.sunk | while | flops 46225860 | bytes 11118722 | solution.py:312
  594.6 14.1 %while.264 = (s32[]{:T(128)}, f32[22,22,64]{2,1,0:T(8,128)S(1)}, f32[49,64]{1,0:T(8,128)S(1)}, bf16[49,64]{1,0:T(8,128)(2,1)S(1)}, f32[16,16,64]{2,1,0:T(8,128)S...) while((s32[]{:T(128)}, f32[22,22,64]{2,1,0:T(8,128)S(1)}, ...), condition=%wide.region_26.25_spmd, body=%wide.region_18.24_spmd.sunk | while | flops 487430 | bytes 3453815 | solution.py:92
  629.9 14.1 %while.264 = (s32[]{:T(128)}, f32[22,22,64]{2,1,0:T(8,128)S(1)}, f32[49,64]{1,0:T(8,128)S(1)}, bf16[49,64]{1,0:T(8,128)(2,1)S(1)}, f32[16,16,64]{2,1,0:T(8,128)S...) while((s32[]{:T(128)}, f32[22,22,64]{2,1,0:T(8,128)S(1)}, ...), condition=%wide.region_26.25_spmd, body=%wide.region_18.24_spmd.sunk | while | flops 487430 | bytes 3453815 | solution.py:92
  668.5 69.7 %while.262 = (s32[]{:T(128)}, bf16[16,16,64]{2,1,0:T(8,128)(2,1)S(1)}, f32[2,49,64]{2,1,0:T(8,128)S(1)}, f32[2,64,256]{2,1,0:T(8,128)S(1)}, f32[2,256,64]{1,2,0:...) while((s32[]{:T(128)}, ...), condition=%wide.region_28.28_spmd, body=%wide.region_11.27_spmd.sunk | while | flops 46225860 | bytes 11118722 | solution.py:312
  672.0 14.1 %while.264 = (s32[]{:T(128)}, f32[22,22,64]{2,1,0:T(8,128)S(1)}, f32[49,64]{1,0:T(8,128)S(1)}, bf16[49,64]{1,0:T(8,128)(2,1)S(1)}, f32[16,16,64]{2,1,0:T(8,128)S...) while((s32[]{:T(128)}, f32[22,22,64]{2,1,0:T(8,128)S(1)}, ...), condition=%wide.region_26.25_spmd, body=%wide.region_18.24_spmd.sunk | while | flops 487430 | bytes 3453815 | solution.py:92
  707.3 14.1 %while.264 = (s32[]{:T(128)}, f32[22,22,64]{2,1,0:T(8,128)S(1)}, f32[49,64]{1,0:T(8,128)S(1)}, bf16[49,64]{1,0:T(8,128)(2,1)S(1)}, f32[16,16,64]{2,1,0:T(8,128)S...) while((s32[]{:T(128)}, f32[22,22,64]{2,1,0:T(8,128)S(1)}, ...), condition=%wide.region_26.25_spmd, body=%wide.region_18.24_spmd.sunk | while | flops 487430 | bytes 3453815 | solution.py:92
  745.9 69.7 %while.262 = (s32[]{:T(128)}, bf16[16,16,64]{2,1,0:T(8,128)(2,1)S(1)}, f32[2,49,64]{2,1,0:T(8,128)S(1)}, f32[2,64,256]{2,1,0:T(8,128)S(1)}, f32[2,256,64]{1,2,0:...) while((s32[]{:T(128)}, ...), condition=%wide.region_28.28_spmd, body=%wide.region_11.27_spmd.sunk | while | flops 46225860 | bytes 11118722 | solution.py:312
  749.4 14.1 %while.264 = (s32[]{:T(128)}, f32[22,22,64]{2,1,0:T(8,128)S(1)}, f32[49,64]{1,0:T(8,128)S(1)}, bf16[49,64]{1,0:T(8,128)(2,1)S(1)}, f32[16,16,64]{2,1,0:T(8,128)S...) while((s32[]{:T(128)}, f32[22,22,64]{2,1,0:T(8,128)S(1)}, ...), condition=%wide.region_26.25_spmd, body=%wide.region_18.24_spmd.sunk | while | flops 487430 | bytes 3453815 | solution.py:92
  784.7 14.1 %while.264 = (s32[]{:T(128)}, f32[22,22,64]{2,1,0:T(8,128)S(1)}, f32[49,64]{1,0:T(8,128)S(1)}, bf16[49,64]{1,0:T(8,128)(2,1)S(1)}, f32[16,16,64]{2,1,0:T(8,128)S...) while((s32[]{:T(128)}, f32[22,22,64]{2,1,0:T(8,128)S(1)}, ...), condition=%wide.region_26.25_spmd, body=%wide.region_18.24_spmd.sunk | while | flops 487430 | bytes 3453815 | solution.py:92
  823.2 28.1 %psum.21 = f32[2,49,64]{2,0,1:T(2,128)S(1)} all-reduce(f32[2,49,64]{2,0,1:T(2,128)S(1)} %copy.89), channel_id=1, replica_groups=mesh['section'=4,'tile'=8] {'tile'}, use_global_device_ids=true, to_apply=%region_31.32 | all-reduce | flops 6272 | bytes 50176 | tf_op jit(solution)/shard_map/psum | solution.py:333
  852.0 26.5 %all-reduce.12.cloned.1.call-done = (f32[2,64,256]{2,1,0:T(8,128)}, f32[2,256,64]{1,2,0:T(8,128)}) async-done(((f32[2,64,256]{2,1,0:T(8,128)}, f32[2,256,64]{1,2,0:T(8,128)}), (f32[2,64,256]{2,1,0:T(8,128)}, f32[2,256,64]{1,2,0:T(8,128)})) %all-reduce.12.cloned.1.call-update) | async-done | bytes 262160 | tf_op jit(solution)/shard_map/psum | solution.py:333
  (5381 shorter events, 809.9 us)
Async XLA Ops:
  7.2 871.3 %all-reduce.12.cloned.1.call-start = ((), (), s32[]{:S(2)}) async-start(), calls=%async_computation | async-start | bytes 524288 | tf_op jit(solution)/shard_map/psum | solution.py:333
  300.2 10.7 %collective-permute-start = (f32[576]{0:T(1024)S(1)}, f32[576]{0:T(1024)S(1)}, u32[]{:S(2)}, u32[]{:S(2)}) collective-permute-start(f32[576]{0:T(1024)S(1)} %get-tuple-element.5111), channel_id=1, source_target_pairs={{0,3},{1,4},{2,5},{3,6},{4,7},{5,0},{6,1},{7,2},{8,11},{9,12},{10,... | collective-permute-start | bytes 6920 | tf_op jit(solution)/shard_map/while/body/eval_jaxpr/while/body/eval_jaxpr/ppermute | solution.py:24
  300.3 10.7 %collective-permute-start.1 = (f32[576]{0:T(1024)S(1)}, f32[576]{0:T(1024)S(1)}, u32[]{:S(2)}, u32[]{:S(2)}) collective-permute-start(f32[576]{0:T(1024)S(1)} %get-tuple-element.5112), channel_id=1, source_target_pairs={{0,3},{1,4},{2,5},{3,6},{4,7},{5,0},{6,1},{7,2},{8,11},{9,12},{10,... | collective-permute-start | bytes 6920 | tf_op jit(solution)/shard_map/while/body/eval_jaxpr/while/body/eval_jaxpr/ppermute | solution.py:24
  301.6 9.9 %collective-permute-start.2 = (f32[576]{0:T(1024)S(1)}, f32[576]{0:T(1024)S(1)}, u32[]{:S(2)}, u32[]{:S(2)}) collective-permute-start(f32[576]{0:T(1024)S(1)} %get-tuple-element.5113), channel_id=1, source_target_pairs={{0,5},{1,6},{2,7},{3,0},{4,1},{5,2},{6,3},{7,4},{8,13},{9,14},{10,... | collective-permute-start | bytes 6920 | tf_op jit(solution)/shard_map/while/body/eval_jaxpr/while/body/eval_jaxpr/ppermute | solution.py:24
  335.1 10.6 %collective-permute-start = (f32[576]{0:T(1024)S(1)}, f32[576]{0:T(1024)S(1)}, u32[]{:S(2)}, u32[]{:S(2)}) collective-permute-start(f32[576]{0:T(1024)S(1)} %get-tuple-element.5111), channel_id=1, source_target_pairs={{0,3},{1,4},{2,5},{3,6},{4,7},{5,0},{6,1},{7,2},{8,11},{9,12},{10,... | collective-permute-start | bytes 6920 | tf_op jit(solution)/shard_map/while/body/eval_jaxpr/while/body/eval_jaxpr/ppermute | solution.py:24
  335.1 10.6 %collective-permute-start.1 = (f32[576]{0:T(1024)S(1)}, f32[576]{0:T(1024)S(1)}, u32[]{:S(2)}, u32[]{:S(2)}) collective-permute-start(f32[576]{0:T(1024)S(1)} %get-tuple-element.5112), channel_id=1, source_target_pairs={{0,3},{1,4},{2,5},{3,6},{4,7},{5,0},{6,1},{7,2},{8,11},{9,12},{10,... | collective-permute-start | bytes 6920 | tf_op jit(solution)/shard_map/while/body/eval_jaxpr/while/body/eval_jaxpr/ppermute | solution.py:24
  336.1 10.1 %collective-permute-start.2 = (f32[576]{0:T(1024)S(1)}, f32[576]{0:T(1024)S(1)}, u32[]{:S(2)}, u32[]{:S(2)}) collective-permute-start(f32[576]{0:T(1024)S(1)} %get-tuple-element.5113), channel_id=1, source_target_pairs={{0,5},{1,6},{2,7},{3,0},{4,1},{5,2},{6,3},{7,4},{8,13},{9,14},{10,... | collective-permute-start | bytes 6920 | tf_op jit(solution)/shard_map/while/body/eval_jaxpr/while/body/eval_jaxpr/ppermute | solution.py:24
  377.2 10.8 %collective-permute-start = (f32[576]{0:T(1024)S(1)}, f32[576]{0:T(1024)S(1)}, u32[]{:S(2)}, u32[]{:S(2)}) collective-permute-start(f32[576]{0:T(1024)S(1)} %get-tuple-element.5111), channel_id=1, source_target_pairs={{0,3},{1,4},{2,5},{3,6},{4,7},{5,0},{6,1},{7,2},{8,11},{9,12},{10,... | collective-permute-start | bytes 6920 | tf_op jit(solution)/shard_map/while/body/eval_jaxpr/while/body/eval_jaxpr/ppermute | solution.py:24
  377.3 10.8 %collective-permute-start.1 = (f32[576]{0:T(1024)S(1)}, f32[576]{0:T(1024)S(1)}, u32[]{:S(2)}, u32[]{:S(2)}) collective-permute-start(f32[576]{0:T(1024)S(1)} %get-tuple-element.5112), channel_id=1, source_target_pairs={{0,3},{1,4},{2,5},{3,6},{4,7},{5,0},{6,1},{7,2},{8,11},{9,12},{10,... | collective-permute-start | bytes 6920 | tf_op jit(solution)/shard_map/while/body/eval_jaxpr/while/body/eval_jaxpr/ppermute | solution.py:24
  412.2 10.4 %collective-permute-start = (f32[576]{0:T(1024)S(1)}, f32[576]{0:T(1024)S(1)}, u32[]{:S(2)}, u32[]{:S(2)}) collective-permute-start(f32[576]{0:T(1024)S(1)} %get-tuple-element.5111), channel_id=1, source_target_pairs={{0,3},{1,4},{2,5},{3,6},{4,7},{5,0},{6,1},{7,2},{8,11},{9,12},{10,... | collective-permute-start | bytes 6920 | tf_op jit(solution)/shard_map/while/body/eval_jaxpr/while/body/eval_jaxpr/ppermute | solution.py:24
  412.3 10.4 %collective-permute-start.1 = (f32[576]{0:T(1024)S(1)}, f32[576]{0:T(1024)S(1)}, u32[]{:S(2)}, u32[]{:S(2)}) collective-permute-start(f32[576]{0:T(1024)S(1)} %get-tuple-element.5112), channel_id=1, source_target_pairs={{0,3},{1,4},{2,5},{3,6},{4,7},{5,0},{6,1},{7,2},{8,11},{9,12},{10,... | collective-permute-start | bytes 6920 | tf_op jit(solution)/shard_map/while/body/eval_jaxpr/while/body/eval_jaxpr/ppermute | solution.py:24
  413.3 9.8 %collective-permute-start.2 = (f32[576]{0:T(1024)S(1)}, f32[576]{0:T(1024)S(1)}, u32[]{:S(2)}, u32[]{:S(2)}) collective-permute-start(f32[576]{0:T(1024)S(1)} %get-tuple-element.5113), channel_id=1, source_target_pairs={{0,5},{1,6},{2,7},{3,0},{4,1},{5,2},{6,3},{7,4},{8,13},{9,14},{10,... | collective-permute-start | bytes 6920 | tf_op jit(solution)/shard_map/while/body/eval_jaxpr/while/body/eval_jaxpr/ppermute | solution.py:24
  454.6 10.9 %collective-permute-start = (f32[576]{0:T(1024)S(1)}, f32[576]{0:T(1024)S(1)}, u32[]{:S(2)}, u32[]{:S(2)}) collective-permute-start(f32[576]{0:T(1024)S(1)} %get-tuple-element.5111), channel_id=1, source_target_pairs={{0,3},{1,4},{2,5},{3,6},{4,7},{5,0},{6,1},{7,2},{8,11},{9,12},{10,... | collective-permute-start | bytes 6920 | tf_op jit(solution)/shard_map/while/body/eval_jaxpr/while/body/eval_jaxpr/ppermute | solution.py:24
  454.6 10.9 %collective-permute-start.1 = (f32[576]{0:T(1024)S(1)}, f32[576]{0:T(1024)S(1)}, u32[]{:S(2)}, u32[]{:S(2)}) collective-permute-start(f32[576]{0:T(1024)S(1)} %get-tuple-element.5112), channel_id=1, source_target_pairs={{0,3},{1,4},{2,5},{3,6},{4,7},{5,0},{6,1},{7,2},{8,11},{9,12},{10,... | collective-permute-start | bytes 6920 | tf_op jit(solution)/shard_map/while/body/eval_jaxpr/while/body/eval_jaxpr/ppermute | solution.py:24
  489.7 10.2 %collective-permute-start = (f32[576]{0:T(1024)S(1)}, f32[576]{0:T(1024)S(1)}, u32[]{:S(2)}, u32[]{:S(2)}) collective-permute-start(f32[576]{0:T(1024)S(1)} %get-tuple-element.5111), channel_id=1, source_target_pairs={{0,3},{1,4},{2,5},{3,6},{4,7},{5,0},{6,1},{7,2},{8,11},{9,12},{10,... | collective-permute-start | bytes 6920 | tf_op jit(solution)/shard_map/while/body/eval_jaxpr/while/body/eval_jaxpr/ppermute | solution.py:24
  489.8 10.4 %collective-permute-start.1 = (f32[576]{0:T(1024)S(1)}, f32[576]{0:T(1024)S(1)}, u32[]{:S(2)}, u32[]{:S(2)}) collective-permute-start(f32[576]{0:T(1024)S(1)} %get-tuple-element.5112), channel_id=1, source_target_pairs={{0,3},{1,4},{2,5},{3,6},{4,7},{5,0},{6,1},{7,2},{8,11},{9,12},{10,... | collective-permute-start | bytes 6920 | tf_op jit(solution)/shard_map/while/body/eval_jaxpr/while/body/eval_jaxpr/ppermute | solution.py:24
  531.9 11.0 %collective-permute-start = (f32[576]{0:T(1024)S(1)}, f32[576]{0:T(1024)S(1)}, u32[]{:S(2)}, u32[]{:S(2)}) collective-permute-start(f32[576]{0:T(1024)S(1)} %get-tuple-element.5111), channel_id=1, source_target_pairs={{0,3},{1,4},{2,5},{3,6},{4,7},{5,0},{6,1},{7,2},{8,11},{9,12},{10,... | collective-permute-start | bytes 6920 | tf_op jit(solution)/shard_map/while/body/eval_jaxpr/while/body/eval_jaxpr/ppermute | solution.py:24
  532.0 11.0 %collective-permute-start.1 = (f32[576]{0:T(1024)S(1)}, f32[576]{0:T(1024)S(1)}, u32[]{:S(2)}, u32[]{:S(2)}) collective-permute-start(f32[576]{0:T(1024)S(1)} %get-tuple-element.5112), channel_id=1, source_target_pairs={{0,3},{1,4},{2,5},{3,6},{4,7},{5,0},{6,1},{7,2},{8,11},{9,12},{10,... | collective-permute-start | bytes 6920 | tf_op jit(solution)/shard_map/while/body/eval_jaxpr/while/body/eval_jaxpr/ppermute | solution.py:24
  567.1 10.2 %collective-permute-start = (f32[576]{0:T(1024)S(1)}, f32[576]{0:T(1024)S(1)}, u32[]{:S(2)}, u32[]{:S(2)}) collective-permute-start(f32[576]{0:T(1024)S(1)} %get-tuple-element.5111), channel_id=1, source_target_pairs={{0,3},{1,4},{2,5},{3,6},{4,7},{5,0},{6,1},{7,2},{8,11},{9,12},{10,... | collective-permute-start | bytes 6920 | tf_op jit(solution)/shard_map/while/body/eval_jaxpr/while/body/eval_jaxpr/ppermute | solution.py:24
  567.2 10.4 %collective-permute-start.1 = (f32[576]{0:T(1024)S(1)}, f32[576]{0:T(1024)S(1)}, u32[]{:S(2)}, u32[]{:S(2)}) collective-permute-start(f32[576]{0:T(1024)S(1)} %get-tuple-element.5112), channel_id=1, source_target_pairs={{0,3},{1,4},{2,5},{3,6},{4,7},{5,0},{6,1},{7,2},{8,11},{9,12},{10,... | collective-permute-start | bytes 6920 | tf_op jit(solution)/shard_map/while/body/eval_jaxpr/while/body/eval_jaxpr/ppermute | solution.py:24
  609.2 11.1 %collective-permute-start = (f32[576]{0:T(1024)S(1)}, f32[576]{0:T(1024)S(1)}, u32[]{:S(2)}, u32[]{:S(2)}) collective-permute-start(f32[576]{0:T(1024)S(1)} %get-tuple-element.5111), channel_id=1, source_target_pairs={{0,3},{1,4},{2,5},{3,6},{4,7},{5,0},{6,1},{7,2},{8,11},{9,12},{10,... | collective-permute-start | bytes 6920 | tf_op jit(solution)/shard_map/while/body/eval_jaxpr/while/body/eval_jaxpr/ppermute | solution.py:24
  609.3 11.1 %collective-permute-start.1 = (f32[576]{0:T(1024)S(1)}, f32[576]{0:T(1024)S(1)}, u32[]{:S(2)}, u32[]{:S(2)}) collective-permute-start(f32[576]{0:T(1024)S(1)} %get-tuple-element.5112), channel_id=1, source_target_pairs={{0,3},{1,4},{2,5},{3,6},{4,7},{5,0},{6,1},{7,2},{8,11},{9,12},{10,... | collective-permute-start | bytes 6920 | tf_op jit(solution)/shard_map/while/body/eval_jaxpr/while/body/eval_jaxpr/ppermute | solution.py:24
  644.5 10.1 %collective-permute-start = (f32[576]{0:T(1024)S(1)}, f32[576]{0:T(1024)S(1)}, u32[]{:S(2)}, u32[]{:S(2)}) collective-permute-start(f32[576]{0:T(1024)S(1)} %get-tuple-element.5111), channel_id=1, source_target_pairs={{0,3},{1,4},{2,5},{3,6},{4,7},{5,0},{6,1},{7,2},{8,11},{9,12},{10,... | collective-permute-start | bytes 6920 | tf_op jit(solution)/shard_map/while/body/eval_jaxpr/while/body/eval_jaxpr/ppermute | solution.py:24
  644.6 10.4 %collective-permute-start.1 = (f32[576]{0:T(1024)S(1)}, f32[576]{0:T(1024)S(1)}, u32[]{:S(2)}, u32[]{:S(2)}) collective-permute-start(f32[576]{0:T(1024)S(1)} %get-tuple-element.5112), channel_id=1, source_target_pairs={{0,3},{1,4},{2,5},{3,6},{4,7},{5,0},{6,1},{7,2},{8,11},{9,12},{10,... | collective-permute-start | bytes 6920 | tf_op jit(solution)/shard_map/while/body/eval_jaxpr/while/body/eval_jaxpr/ppermute | solution.py:24
  686.6 11.1 %collective-permute-start = (f32[576]{0:T(1024)S(1)}, f32[576]{0:T(1024)S(1)}, u32[]{:S(2)}, u32[]{:S(2)}) collective-permute-start(f32[576]{0:T(1024)S(1)} %get-tuple-element.5111), channel_id=1, source_target_pairs={{0,3},{1,4},{2,5},{3,6},{4,7},{5,0},{6,1},{7,2},{8,11},{9,12},{10,... | collective-permute-start | bytes 6920 | tf_op jit(solution)/shard_map/while/body/eval_jaxpr/while/body/eval_jaxpr/ppermute | solution.py:24
  686.7 11.1 %collective-permute-start.1 = (f32[576]{0:T(1024)S(1)}, f32[576]{0:T(1024)S(1)}, u32[]{:S(2)}, u32[]{:S(2)}) collective-permute-start(f32[576]{0:T(1024)S(1)} %get-tuple-element.5112), channel_id=1, source_target_pairs={{0,3},{1,4},{2,5},{3,6},{4,7},{5,0},{6,1},{7,2},{8,11},{9,12},{10,... | collective-permute-start | bytes 6920 | tf_op jit(solution)/shard_map/while/body/eval_jaxpr/while/body/eval_jaxpr/ppermute | solution.py:24
  721.9 10.0 %collective-permute-start = (f32[576]{0:T(1024)S(1)}, f32[576]{0:T(1024)S(1)}, u32[]{:S(2)}, u32[]{:S(2)}) collective-permute-start(f32[576]{0:T(1024)S(1)} %get-tuple-element.5111), channel_id=1, source_target_pairs={{0,3},{1,4},{2,5},{3,6},{4,7},{5,0},{6,1},{7,2},{8,11},{9,12},{10,... | collective-permute-start | bytes 6920 | tf_op jit(solution)/shard_map/while/body/eval_jaxpr/while/body/eval_jaxpr/ppermute | solution.py:24
  722.0 10.4 %collective-permute-start.1 = (f32[576]{0:T(1024)S(1)}, f32[576]{0:T(1024)S(1)}, u32[]{:S(2)}, u32[]{:S(2)}) collective-permute-start(f32[576]{0:T(1024)S(1)} %get-tuple-element.5112), channel_id=1, source_target_pairs={{0,3},{1,4},{2,5},{3,6},{4,7},{5,0},{6,1},{7,2},{8,11},{9,12},{10,... | collective-permute-start | bytes 6920 | tf_op jit(solution)/shard_map/while/body/eval_jaxpr/while/body/eval_jaxpr/ppermute | solution.py:24
  764.0 11.1 %collective-permute-start = (f32[576]{0:T(1024)S(1)}, f32[576]{0:T(1024)S(1)}, u32[]{:S(2)}, u32[]{:S(2)}) collective-permute-start(f32[576]{0:T(1024)S(1)} %get-tuple-element.5111), channel_id=1, source_target_pairs={{0,3},{1,4},{2,5},{3,6},{4,7},{5,0},{6,1},{7,2},{8,11},{9,12},{10,... | collective-permute-start | bytes 6920 | tf_op jit(solution)/shard_map/while/body/eval_jaxpr/while/body/eval_jaxpr/ppermute | solution.py:24
  764.1 11.1 %collective-permute-start.1 = (f32[576]{0:T(1024)S(1)}, f32[576]{0:T(1024)S(1)}, u32[]{:S(2)}, u32[]{:S(2)}) collective-permute-start(f32[576]{0:T(1024)S(1)} %get-tuple-element.5112), channel_id=1, source_target_pairs={{0,3},{1,4},{2,5},{3,6},{4,7},{5,0},{6,1},{7,2},{8,11},{9,12},{10,... | collective-permute-start | bytes 6920 | tf_op jit(solution)/shard_map/while/body/eval_jaxpr/while/body/eval_jaxpr/ppermute | solution.py:24
  799.4 10.1 %collective-permute-start = (f32[576]{0:T(1024)S(1)}, f32[576]{0:T(1024)S(1)}, u32[]{:S(2)}, u32[]{:S(2)}) collective-permute-start(f32[576]{0:T(1024)S(1)} %get-tuple-element.5111), channel_id=1, source_target_pairs={{0,3},{1,4},{2,5},{3,6},{4,7},{5,0},{6,1},{7,2},{8,11},{9,12},{10,... | collective-permute-start | bytes 6920 | tf_op jit(solution)/shard_map/while/body/eval_jaxpr/while/body/eval_jaxpr/ppermute | solution.py:24
  799.4 10.4 %collective-permute-start.1 = (f32[576]{0:T(1024)S(1)}, f32[576]{0:T(1024)S(1)}, u32[]{:S(2)}, u32[]{:S(2)}) collective-permute-start(f32[576]{0:T(1024)S(1)} %get-tuple-element.5112), channel_id=1, source_target_pairs={{0,3},{1,4},{2,5},{3,6},{4,7},{5,0},{6,1},{7,2},{8,11},{9,12},{10,... | collective-permute-start | bytes 6920 | tf_op jit(solution)/shard_map/while/body/eval_jaxpr/while/body/eval_jaxpr/ppermute | solution.py:24
  (173 other events, 1290.5 us)
Sparse Core Ops, SparseCore 0:
  823.3 55.0 all-reduce.11
where the time goes:
time: 891 us; the launch traced here: 888 us
  local copies, waits for them, and re-layouts  207 us (23%)
  starting transfers between devices  205 us (23%)
  other arithmetic  193 us (22%)
  waiting for transfers between devices  145 us (16%)
  matrix products  38.7 us (4%)
  between operations  35.8 us (4%)
  loops' own time  35.2 us (4%)
  blocking collectives  28.1 us (3%)
    ppermute x182, starting transfers between devices, from_behind(): return lax.ppermute(value, axis, pairs)  166 us
    scatter-add x686, local copies, waits for them, and re-layouts, row_step(): spread_rows.at[:, tap_col:tap_col + extent, :]  128 us
    ppermute x182, waiting for transfers between devices, from_behind(): return lax.ppermute(value, axis, pairs)  96.4 us
    another operation x42, other arithmetic  39.5 us
    ppermute x14, starting transfers between devices, shifted(): return lax.ppermute(shard, axis, pairs)  38.4 us
    add x196, other arithmetic, row_step(): accum_total + band[:, tap_col:tap_col + extent, :] * row_taps[tap_col]  28.5 us
    psum x1, blocking collectives, on_device(): lax.psum((local_sums[0], local_sums[1], local_sums[2]), 'tile')  28.1 us
    psum x1, waiting for transfers between devices, on_device(): lax.psum((local_sums[0], local_sums[1], local_sums[2]), 'tile')  26.5 us

commit v1 on v0

v1 whole, which is shorter than its diff:
```python
import functools
import math

import jax
import jax.numpy as jnp
from jax import lax
from jax.experimental import pallas as pl
from jax.experimental.pallas import tpu as pltpu
from jax.sharding import PartitionSpec as P

norm_eps = 1e-06
rim = 3
side = 7
gelu_k = math.sqrt(2.0 / math.pi)
gelu_c = 0.044715
f32, bf16 = jnp.float32, jnp.bfloat16
WEST, EAST = 0, 1


def grid_offsets(tile_count):
    columns = max(tile_count // 8, 4)
    return [-columns, 1, columns, -1, 1 - columns, columns + 1, columns - 1, -columns - 1]


def unpacked(v):
    half = v.shape[1] // 2
    return jnp.concatenate([v[:, :half], v[:, half:]], axis=0)


def packed(v):
    half = v.shape[0] // 2
    return jnp.concatenate([v[:half], v[half:]], axis=1)


def mm(a, b, dims):
    return lax.dot_general(a, b, ((dims[0], dims[1]), ((), ())), preferred_element_type=f32)


def half_mean(v, averaging):
    high = v.astype(bf16)
    low = (v - high.astype(f32)).astype(bf16)
    return mm(jnp.concatenate([high, low], axis=1), averaging, ((1,), (0,)))


def kernel(
    tile_count,
    layers,
    x_ref,
    ct_ref,
    taps_ref,
    w1_ref,
    w2_ref,
    mask_ref,
    zo_ref,
    go_ref,
    dk_ref,
    dw1_ref,
    dw2_ref,
    pad,
    odd,
    es,
    fr,
    xhat,
    inv,
    us,
    gs,
    slope,
    dz,
    dodd,
    dp,
    eb,
    br,
    bn,
    field,
    grad,
    averaging,
    send_sem,
    frecv,
    brecv,
):
    me = lax.axis_index("tile")
    offsets = grid_offsets(tile_count)
    north, east, south, west, ne, se, sw, nw = [
        lax.rem(me + (off % tile_count), tile_count) for off in offsets
    ]

    def copies(plan, recv):
        return [
            pltpu.make_async_remote_copy(
                src_ref=src,
                dst_ref=dst,
                send_sem=send_sem.at[i],
                recv_sem=recv.at[i],
                device_id={"tile": target},
                device_id_type=pl.DeviceIdType.MESH,
            )
            for i, (target, src, dst) in enumerate(plan)
        ]

    def forward_copies(l):
        return copies(
            [
                (north, pad.at[l, 3:6, 8:16], pad.at[l, 19:22, 8:16]),
                (south, pad.at[l, 16:19, 8:16], pad.at[l, 0:3, 8:16]),
                (nw, es.at[WEST, :, 0:8], fr.at[l, EAST, :, 24:32]),
                (ne, es.at[EAST, :, 0:8], fr.at[l, WEST, :, 24:32]),
                (se, es.at[EAST, :, 8:16], fr.at[l, WEST, :, 0:8]),
                (sw, es.at[WEST, :, 8:16], fr.at[l, EAST, :, 0:8]),
                (east, es.at[EAST], fr.at[l, WEST, :, 8:24]),
                (west, es.at[WEST], fr.at[l, EAST, :, 8:24]),
            ],
            frecv.at[l],
        )

    def backward_copies(l):
        return copies(
            [
                (north, dp.at[0:3, 8:16], bn.at[l, 1]),
                (south, dp.at[19:22, 8:16], bn.at[l, 0]),
                (nw, eb.at[WEST, :, 0:8], br.at[l, EAST, :, 24:32]),
                (ne, eb.at[EAST, :, 0:8], br.at[l, WEST, :, 24:32]),
                (se, eb.at[EAST, :, 24:32], br.at[l, WEST, :, 16:24]),
                (sw, eb.at[WEST, :, 24:32], br.at[l, EAST, :, 16:24]),
                (east, eb.at[EAST, :, 8:24], br.at[l, WEST, :, 0:16]),
                (west, eb.at[WEST, :, 8:24], br.at[l, EAST, :, 0:16]),
            ],
            brecv.at[l],
        )

    def offer(l, z):
        pad[l, 3:19, 8:16, :] = z.reshape(16, 8, 128)
        field[...] = z
        for pair in range(2):
            es[WEST, pair] = field[pl.ds(pair, 16, stride=8), :]
            es[EAST, pair] = field[pl.ds(6 + pair, 16, stride=8), :]

    barrier = pltpu.get_barrier_semaphore()
    partners = sorted({off % tile_count for off in offsets})
    for off in partners:
        pl.semaphore_signal(
            barrier,
            inc=1,
            device_id={"tile": lax.rem(me + off, tile_count)},
            device_id_type=pl.DeviceIdType.MESH,
        )

    offer(0, x_ref[...])
    rows = lax.broadcasted_iota(jnp.int32, (256, 128), 0)
    lanes = lax.broadcasted_iota(jnp.int32, (256, 128), 1)
    same = ((rows % 128) < 64) == (lanes < 64)
    averaging[...] = jnp.where(same, 1.0 / 64.0, 0.0).astype(bf16)
    dz[...] = jnp.zeros_like(dz)
    dodd[...] = jnp.zeros_like(dodd)
    eb[...] = jnp.zeros_like(eb)
    pl.semaphore_wait(barrier, len(partners))
    for copy in forward_copies(0):
        copy.start()

    def low_lanes(shape):
        return lax.broadcasted_iota(jnp.int32, shape, len(shape) - 1) < 64

    def forward_step(l, carry):
        sent = forward_copies(l)
        for copy in sent:
            copy.wait_recv()
        for edge in range(2):
            for pair in range(2):
                column = fr[l, edge, pair, 5:27, :] * mask_ref[edge]
                place = (6 if edge == WEST else 16) + pair
                pad[l, :, place : place + 1, :] = column.reshape(22, 1, 128)
        keep = low_lanes((22, 16, 128))
        merged = jnp.where(keep, pad[l, :, 7:23, :], pad[l, :, 6:22, :])
        odd[l] = pltpu.roll(merged.reshape(22 * 16, 128), 64, 1).reshape(22, 16, 128)
        total = jnp.zeros((16, 8, 128), f32)
        for a in range(side):
            for b in range(side):
                if b % 2:
                    start = 6 + (b + 1) // 2
                    window = pad[l, a : a + 16, start : start + 8, :]
                else:
                    window = odd[l, a : a + 16, b // 2 : b // 2 + 8, :]
                total = total + window * taps_ref[l, side * a + b]
        h = total.reshape(128, 128)
        avg = averaging[...]
        centred = h - half_mean(h, avg)
        scale = lax.rsqrt(half_mean(centred * centred, avg) + norm_eps)
        normed = centred * scale
        xhat[l] = normed
        inv[l] = scale
        u = unpacked(normed.astype(bf16))
        us[l] = u
        before = mm(u, w1_ref[l], ((1,), (0,)))
        t = jnp.tanh(gelu_k * (before + gelu_c * before * before * before))
        g = (0.5 * before * (1.0 + t)).astype(bf16)
        gs[l] = g
        branch = packed(mm(g, w2_ref[l], ((1,), (0,))))
        z = pad[l, 3:19, 8:16, :].reshape(128, 128) + branch
        z16 = z.astype(bf16)
        zo_ref[l // 2] = z16
        for copy in sent:
            copy.wait_send()

        @pl.when(l < layers - 1)
        def _():
            offer(l + 1, z16.astype(f32))
            for copy in forward_copies(l + 1):
                copy.start()

        square = before * before
        slope[l] = 0.5 * (1.0 + t) + 0.5 * before * (1.0 - t * t) * gelu_k * (
            1.0 + 3.0 * gelu_c * square
        )
        return carry

    lax.fori_loop(0, layers, forward_step, 0)

    grad[...] = ct_ref[...]

    def backward_step(count, carry):
        l = layers - 1 - count
        d = grad[...]
        d_rows = unpacked(d.astype(bf16))
        dg = mm(d_rows, w2_ref[l], ((1,), (1,)))
        da = (dg * slope[l]).astype(bf16)
        du = packed(mm(da, w1_ref[l], ((1,), (1,))))
        avg = averaging[...]
        normed = xhat[l]
        dh = inv[l] * (du - half_mean(du, avg) - normed * half_mean(du * normed, avg))
        dh3 = dh.reshape(16, 8, 128)
        dz[6:22, 8:16, :] = dh3
        keep = low_lanes((16, 8, 128))
        for start in (0, 8):
            merged = jnp.where(
                keep, dz[6:22, start + 1 : start + 9, :], dz[6:22, start : start + 8, :]
            )
            rolled = pltpu.roll(merged.reshape(128, 128), 64, 1).reshape(16, 8, 128)
            dodd[6:22, start : start + 8, :] = rolled
        for top in (0, 11):
            total = jnp.zeros((11, 16, 128), f32)
            for a in range(side):
                for b in range(side):
                    shift = 3 - b
                    first = top + 6 - a
                    if shift % 2 == 0:
                        start = 6 + shift // 2
                        window = dz[first : first + 11, start : start + 16, :]
                    else:
                        start = 6 + (shift - 1) // 2
                        window = dodd[first : first + 11, start : start + 16, :]
                    total = total + window * taps_ref[l, side * a + b]
            dp[top : top + 11, 6:22, :] = total
        for edge in range(2):
            for pair in range(2):
                place = (6 if edge == WEST else 16) + pair
                column = dp[:, place : place + 1, :].reshape(22, 128)
                eb[edge, pair, 5:27, :] = column * mask_ref[edge]
        sent = backward_copies(l)
        for copy in sent:
            copy.start()

        for a in range(side):
            for b in range(side):
                if b % 2:
                    start = 6 + (b + 1) // 2
                    window = pad[l, a : a + 16, start : start + 8, :]
                else:
                    window = odd[l, a : a + 16, b // 2 : b // 2 + 8, :]
                part = jnp.sum(window * dh3, axis=0)
                dk_ref[l, side * a + b : side * a + b + 1, :] = jnp.sum(
                    part, axis=0, keepdims=True
                )
        dw1_ref[l] = mm(us[l], da, ((0,), (0,)))
        dw2_ref[l] = mm(gs[l], d_rows, ((0,), (0,)))

        for copy in sent:
            copy.wait_recv()
        base = d.reshape(16, 8, 128) + dp[3:19, 8:16, :]
        top_part = base[0:3] + bn[l, 0]
        bottom_part = base[13:16] + bn[l, 1]
        field[...] = jnp.concatenate([top_part, base[3:13], bottom_part], axis=0).reshape(128, 128)
        for edge in range(2):
            for pair in range(2):
                place = (0 if edge == WEST else 6) + pair
                extra = br[l, edge, pair, 0:16, :] + br[l, edge, pair, 16:32, :]
                field[pl.ds(place, 16, stride=8), :] = (
                    field[pl.ds(place, 16, stride=8), :] + extra
                )
        result = field[...].astype(bf16)
        go_ref[l // 2] = result
        grad[...] = result.astype(f32)
        for copy in sent:
            copy.wait_send()
        return carry

    lax.fori_loop(0, layers, backward_step, 0)


def turned(n, code):
    cells = jnp.arange(n * n, dtype=jnp.int32)
    r, c = cells // n, cells % n
    choices = [r * n + c, c * n + (n - 1 - r), (n - 1 - r) * n + (n - 1 - c), (n - 1 - c) * n + r]
    source = choices[0]
    for k in range(1, 4):
        source = jnp.where(code == k, choices[k], source)
    return (source[:, None] == cells[None, :])


def on_device(inputs, cotangent, depth_weight, in_weight, out_weight, neighbours, orientation):
    micro_count, _, extent, merged = inputs.shape
    blocks, taps, channels = depth_weight.shape
    hidden = in_weight.shape[2]
    tile_count = lax.axis_size("tile")
    sections = lax.axis_size("section")
    layers = blocks * sections
    section_id = lax.axis_index("section")
    code = orientation[lax.axis_index("tile")]
    back_code = (-code) % 4
    grad_scale = 1.0 / math.sqrt(micro_count * tile_count * extent * extent)
    pixels = extent * extent

    mine = jnp.stack([inputs[:, 0], cotangent[:, 0]])
    mine = lax.dynamic_index_in_dim(mine, section_id, 1, keepdims=False)
    into = turned(extent, back_code).astype(bf16)
    mine = jnp.einsum(
        "pq,fqc->fpc", into, mine.reshape(2, pixels, channels), preferred_element_type=f32
    )
    mine = mine.reshape(2, pixels // 2, 2 * channels)

    depth_all = lax.all_gather(depth_weight, "section", axis=0, tiled=True)
    in_all = lax.all_gather(in_weight, "section", axis=0, tiled=True)
    out_all = lax.all_gather(out_weight, "section", axis=0, tiled=True)
    taps_turn = turned(side, back_code)
    taps_all = jnp.einsum(
        "pq,lqc->lpc", taps_turn.astype(bf16), depth_all, preferred_element_type=f32
    )
    taps_all = jnp.concatenate([taps_all, taps_all], axis=2)

    ne_ok = (neighbours[0, 4 + back_code] >= 0).astype(f32)
    sw_ok = (neighbours[0, 4 + (2 - code) % 4] >= 0).astype(f32)
    rows = jnp.arange(extent + 2 * rim)
    mask = jnp.stack([jnp.where(rows >= 19, sw_ok, 1.0), jnp.where(rows < 3, ne_ok, 1.0)])
    mask = jnp.broadcast_to(mask[:, :, None], (2, extent + 2 * rim, 128))

    vmem = pl.BlockSpec(memory_space=pltpu.VMEM)
    zo, go, dk, dw1, dw2 = pl.pallas_call(
        functools.partial(kernel, tile_count, layers),
        out_shape=(
            jax.ShapeDtypeStruct((sections, 128, 128), bf16),
            jax.ShapeDtypeStruct((sections, 128, 128), bf16),
            jax.ShapeDtypeStruct((layers, taps, 128), f32),
            jax.ShapeDtypeStruct((layers, channels, hidden), f32),
            jax.ShapeDtypeStruct((layers, hidden, channels), f32),
        ),
        in_specs=[vmem] * 6,
        out_specs=(vmem,) * 5,
        scratch_shapes=[
            pltpu.VMEM((layers, 22, 24, 128), f32),
            pltpu.VMEM((layers, 22, 16, 128), f32),
            pltpu.VMEM((2, 2, 16, 128), f32),
            pltpu.VMEM((layers, 2, 2, 32, 128), f32),
            pltpu.VMEM((layers, 128, 128), f32),
            pltpu.VMEM((layers, 128, 128), f32),
            pltpu.VMEM((layers, 256, 64), bf16),
            pltpu.VMEM((layers, 256, 256), bf16),
            pltpu.VMEM((layers, 256, 256), f32),
            pltpu.VMEM((28, 24, 128), f32),
            pltpu.VMEM((28, 24, 128), f32),
            pltpu.VMEM((22, 24, 128), f32),
            pltpu.VMEM((2, 2, 32, 128), f32),
            pltpu.VMEM((layers, 2, 2, 32, 128), f32),
            pltpu.VMEM((layers, 2, 3, 8, 128), f32),
            pltpu.VMEM((128, 128), f32),
            pltpu.VMEM((128, 128), f32),
            pltpu.VMEM((256, 128), bf16),
            pltpu.SemaphoreType.DMA((8,)),
            pltpu.SemaphoreType.DMA((layers, 8)),
            pltpu.SemaphoreType.DMA((layers, 8)),
        ],
        compiler_params=pltpu.CompilerParams(
            collective_id=0, has_side_effects=True, vmem_limit_bytes=40 * 1024 * 1024
        ),
    )(mine[0], mine[1], taps_all, in_all, out_all, mask)

    fields = jnp.stack([zo, go], axis=1).reshape(sections, 2, pixels, channels)
    outward = turned(extent, code).astype(bf16)
    fields = jnp.einsum("pq,sfqc->sfpc", outward, fields, preferred_element_type=f32).astype(bf16)
    fields = lax.all_to_all(fields, "section", 0, 0, tiled=True)
    section_outputs = fields[:, 0].reshape(1, micro_count, 1, extent, merged)
    section_grads = fields[:, 1].reshape(1, micro_count, 1, extent, merged)

    dk = dk[:, :, :channels] + dk[:, :, channels:]
    dk = jnp.einsum(
        "pq,lqc->lpc",
        turned(side, code).astype(f32),
        dk,
        precision=lax.Precision.HIGHEST,
        preferred_element_type=f32,
    )
    sums = jnp.concatenate(
        [dk.reshape(layers, -1), dw1.reshape(layers, -1), dw2.reshape(layers, -1)], axis=1
    )
    sums = lax.psum_scatter(sums, "section", scatter_dimension=0, tiled=True)
    sums = lax.psum(sums, "tile") * grad_scale
    cut1 = taps * channels
    cut2 = cut1 + channels * hidden
    return (
        section_outputs,
        section_grads,
        sums[:, :cut1].reshape(blocks, taps, channels),
        sums[:, cut1:cut2].reshape(blocks, channels, hidden),
        sums[:, cut2:].reshape(blocks, hidden, channels),
    )


def solution(mesh):
    in_specs = (
        P(None, "tile", None, None),
        P(None, "tile", None, None),
        P("section", None, None),
        P("section", None, None),
        P("section", None, None),
        P("tile", None),
        P(),
    )
    out_specs = (
        P("section", None, "tile", None, None),
        P("section", None, "tile", None, None),
        P("section", None, None),
        P("section", None, None),
        P("section", None, None),
    )
    return jax.shard_map(
        on_device, mesh=mesh, in_specs=in_specs, out_specs=out_specs, check_vma=False
    )
```

time: 891 us -> 267 us (0.30)
  starting transfers between devices: 205 us -> 3.48 us
  other arithmetic: 193 us -> 2.07 us
  local copies, waits for them, and re-layouts: 207 us -> 20.4 us
  Pallas kernels: 0 us -> 90.7 us
  waiting for transfers between devices: 145 us -> 100 us
  matrix products: 38.7 us -> 1.88 us
  loops' own time: 35.2 us -> 0 us
  between operations: 35.8 us -> 20.2 us
    ppermute x196 -> x0, starting transfers between devices: 205 us -> none  [the longest x182 166 us: from_behind(): return lax.ppermute(value, axis, pairs)]
    scatter-add x686 -> x0, local copies, waits for them, and re-layouts: 128 us -> none  [row_step(): spread_rows.at[:, tap_col:tap_col + extent, :]]
    ppermute x196 -> x0, waiting for transfers between devices: 119 us -> none  [the longest x182 96.4 us: from_behind(): return lax.ppermute(value, axis, pairs)]
    pallas_call x0 -> x1, Pallas kernels: none -> 90.7 us  [on_device(): pl.pallas_call(functools.partial(kernel, tile_count, layers), out_shape=(...]
    unnamed x1 -> x3, waiting for transfers between devices: 0.02 us -> 48.6 us
    add x714 -> x0, other arithmetic: 45.4 us -> none  [the longest x196 28.5 us: row_step(): accum_total + band[:, tap_col:tap_col + extent, :] * row_taps[tap_col]]
    another operation x126 -> x2, other arithmetic: 43 us -> 0.79 us  [the longest x1 0.78 us: on_device(): mine = jnp.stack([inputs[:, 0], cotangent[:, 0]])]
    dot_general x98 -> x4, matrix products: 38.7 us -> 1.88 us  [the longest x1 1.07 us: on_device(): jnp.einsum('pq,sfqc->sfpc', outward, fields, preferred_element_type=f32)]
where the time goes in v1:
time: 267 us; the launch traced here: 266 us
  waiting for transfers between devices  100 us (37%)
  Pallas kernels  90.7 us (34%)
  blocking collectives  27.2 us (10%)
  local copies, waits for them, and re-layouts  20.4 us (8%)
  between operations  20.2 us (8%)
  starting transfers between devices  3.48 us (1%)
    pallas_call x1, Pallas kernels, on_device(): pl.pallas_call(functools.partial(kernel, tile_count, layers), out_shape=(...  90.7 us
    psum x1, waiting for transfers between devices, on_device(): sums = lax.psum(sums, 'tile') * grad_scale  51.5 us
    unnamed x3, waiting for transfers between devices  48.6 us
    unnamed x15, local copies, waits for them, and re-layouts  10.7 us
    all_gather x1, blocking collectives, on_device(): depth_all = lax.all_gather(depth_weight, 'section', axis=0, tiled=True)  9.92 us
    all_gather x1, blocking collectives, on_device(): in_all = lax.all_gather(in_weight, 'section', axis=0, tiled=True)  8.97 us
    all_gather x1, blocking collectives, on_device(): out_all = lax.all_gather(out_weight, 'section', axis=0, tiled=True)  8.35 us
  transfers between devices with their start and end apart: 3, of which 2 were waited for; matrix products, arithmetic and copies ran while one was open for 2% of the time, Pallas kernels for 0%

profile of v1, /device:TPU:0, one launch (start us, length us, event | category | flops | bytes accessed | tf_op | source)
XLA Modules:
  0.0 266.1 jit_solution(15373096582992287217)
XLA Ops:
  7.2 1.2 dynamic_slice.14
  12.5 1.3 constant_dynamic-slice_fusion.1
  15.1 0.7 copy.34
  15.8 0.8 fusion.13
  16.8 0.3 convolution_bitcast_fusion.2
  17.3 9.9 %all_gather.9 = bf16[8,49,64]{2,1,0:T(8,128)(2,1)S(1)} all-gather(bf16[2,49,64]{2,1,0:T(8,128)(2,1)S(1)} %copy.34), channel_id=1, replica_groups=mesh['section'=4,'tile'=8] {'section'}, dimensions={0}, use_global_device_ids=true | all-gather | bytes 62720 | tf_op jit(solution)/shard_map/all_gather | solution.py:329
  27.2 0.2 convolution_bitcast_fusion.1
  27.7 9.0 %all_gather.10.w1_ref = bf16[8,64,256]{2,1,0:T(8,128)(2,1)S(1)} all-gather(bf16[2,64,256]{2,1,0:T(8,128)(2,1)S(1)} %copy-done), channel_id=1, replica_groups=mesh['section'=4,'tile'=8] {'section'}, dimensions={0}, use_global_device_ids=true | all-gather | bytes 327680 | tf_op jit(solution)/shard_map/all_gather | solution.py:330
  36.7 8.4 %all_gather.11 = bf16[8,256,64]{1,2,0:T(8,128)(2,1)S(1)} all-gather(bf16[2,256,64]{1,2,0:T(8,128)(2,1)S(1)} %copy-done.1), channel_id=1, replica_groups=mesh['section'=4,'tile'=8] {'section'}, dimensions={0}, use_global_device_ids=true | all-gather | bytes 327680 | tf_op jit(solution)/shard_map/all_gather | solution.py:331
  45.1 0.3 copy.35.w2_ref
  45.4 90.7 %shard_map.110 = (bf16[4,128,128]{2,1,0:T(8,128)(2,1)S(1)}, bf16[4,128,128]{2,1,0:T(8,128)(2,1)S(1)}, f32[8,49,128]{2,1,0:T(8,128)S(1)}, f32[8,64,256]{2,1,0:T(8,128)S(1)}, f32[8,256,64]{2,1,0:T(8,128)S(1)}) custom-call(f32[128,128]{1,0:T(8,128)S(1)} %squeeze.14.x_ref, f32[128,128]{1,0:T(8,128)S(1)} %squeeze.15.ct_ref, ...), custom_call_target="tpu_custom_call" | custom-call | tf_op jit(solution)/shard_map/pallas_call | solution.py:345
  136.2 0.3 convolution_bitcast_fusion
  136.7 0.3 copy.46
  137.0 0.4 reshape.147
  137.3 1.8 dynamic-update-slice
  139.1 3.1 %dynamic-update-slice.1 = f32[8,35904]{1,0:T(8,128)} dynamic-update-slice(f32[8,35904]{1,0:T(8,128)} %dynamic-update-slice, f32[8,16384]{1,0:T(8,128)S(1)} %bitcast.49, s32[]{} %constant.122, s32[]{} %constant.123) | dynamic-update-slice | bytes 1048580
  142.2 2.6 dynamic-update-slice.2
  145.4 1.1 fusion
  146.4 3.4 %all-to-all-start = ((bf16[4,2,256,64]{2,3,1,0:T(8,128)(2,1)}), bf16[4,2,256,64]{2,3,1,0:T(8,128)(2,1)S(1)}, u32[]{:S(2)}, u32[]{:S(2)}) async-start(bf16[4,2,256,64]{2,3,1,0:T(8,128)(2,1)} %fusion), calls=%async_computation | async-start | bytes 524288 | tf_op jit(solution)/shard_map/all_to_all | solution.py:387
  149.9 0.6 dynamic-slice
  151.2 48.5 %all-reduce.6.cloned.1.call-done = f32[8,35904]{1,0:T(8,128)} async-done(((f32[8,35904]{1,0:T(8,128)}), f32[8,35904]{1,0:T(8,128)}) %all-reduce.6.cloned.1.call-update) | async-done | bytes 1148944
  199.7 2.1 constant_dynamic-slice_fusion.2
  201.8 0.2 copy.39
  202.0 0.9 reshape_squeeze.7
  203.1 0.9 reshape_squeeze.6
  203.9 51.5 %all-reduce.4.cloned.1.call-done = f32[2,35904]{1,0:T(2,128)} async-done(((f32[2,35904]{1,0:T(2,128)}), f32[2,35904]{1,0:T(2,128)}) %all-reduce.4.cloned.1.call-update) | async-done | bytes 287248 | tf_op jit(solution)/shard_map/psum | solution.py:403
  255.4 1.1 broadcast_multiply_fusion
  256.5 0.3 fusion.23
  256.8 0.7 copy.49
  257.6 0.6 copy.42
  258.3 0.2 reshape.150
  258.5 0.8 copy.43
  (34 shorter events, 1.8 us)
Async XLA Ops:
  7.2 192.5 %all-reduce.6.cloned.1.call-start = ((), (), s32[]{:S(2)}) async-start(), calls=%async_computation.2 | async-start | bytes 2301952
  16.8 11.0 %copy-start = (bf16[2,64,256]{2,1,0:T(8,128)(2,1)S(1)}, bf16[2,64,256]{2,1,0:T(8,128)(2,1)}, u32[]{:S(2)}) copy-start(bf16[2,64,256]{2,1,0:T(8,128)(2,1)} %param.10) | copy-start | bytes 196612
  17.0 19.7 %copy-start.1 = (bf16[2,256,64]{1,2,0:T(8,128)(2,1)S(1)}, bf16[2,256,64]{1,2,0:T(8,128)(2,1)}, u32[]{:S(2)}) copy-start(bf16[2,256,64]{1,2,0:T(8,128)(2,1)} %param.11) | copy-start | bytes 196612
  145.0 5.0 %copy-start.2 = (u32[32]{0:T(128)S(1)}, u32[32]{0:T(128)}, u32[]{:S(2)}) copy-start(u32[32]{0:T(128)} %constant.120) | copy-start | bytes 388
  146.4 55.4 %all-to-all-start = ((bf16[4,2,256,64]{2,3,1,0:T(8,128)(2,1)}), bf16[4,2,256,64]{2,3,1,0:T(8,128)(2,1)S(1)}, u32[]{:S(2)}, u32[]{:S(2)}) async-start(bf16[4,2,256,64]{2,3,1,0:T(8,128)(2,1)} %fusion), calls=%async_computation | async-start | bytes 524288 | tf_op jit(solution)/shard_map/all_to_all | solution.py:387
  149.9 105.5 %all-reduce.4.cloned.1.call-start = ((), (), s32[]{:S(2)}) async-start(), calls=%async_computation.1 | async-start | bytes 575488 | tf_op jit(solution)/shard_map/psum | solution.py:403
Sparse Core Ops, SparseCore 0:
  144.9 54.7 all-reduce.5
  202.1 53.1 all-reduce.3

commit v2 on v1

--- a/solution.py
+++ b/solution.py
@@ -44,18 +44,38 @@
 
 def kernel(
     tile_count,
-    layers,
+    sections,
+    blocks,
+    piece,
+    grad_scale,
     x_ref,
     ct_ref,
+    taps_own,
+    w1_own,
+    w2_own,
+    mask_ref,
+    perm_ref,
+    tap_perm_ref,
+    zo_ref,
+    go_ref,
+    dk_out,
+    dw1_out,
+    dw2_out,
+    taps_raw,
     taps_ref,
     w1_ref,
     w2_ref,
-    mask_ref,
-    zo_ref,
-    go_ref,
+    zst,
+    gst,
+    zrec,
+    grec,
+    out_field,
     dk_ref,
-    dw1_ref,
-    dw2_ref,
+    part,
+    arec,
+    total_ref,
+    rs,
+    fin,
     pad,
     odd,
     es,
@@ -77,8 +97,62 @@
     send_sem,
     frecv,
     brecv,
+    wsend,
+    wrecv,
+    zsend,
+    zrecv,
+    gsend,
+    grecv,
+    asend,
+    arecv,
+    rsend,
+    rrecv,
+    csend,
+    crecv,
 ):
+    layers = sections * blocks
     me = lax.axis_index("tile")
+    mine = lax.axis_index("section")
+    others = [lax.rem(mine + k, sections) for k in range(1, sections)]
+
+    def across(axis, target, src, dst, send, recv):
+        return pltpu.make_async_remote_copy(
+            src_ref=src,
+            dst_ref=dst,
+            send_sem=send,
+            recv_sem=recv,
+            device_id={axis: target},
+            device_id_type=pl.DeviceIdType.MESH,
+        )
+
+    def weight_copies(target, source):
+        return [
+            across("section", target, ref.at[source], ref.at[source], wsend.at[target, i], wrecv.at[source, i])
+            for i, ref in enumerate((taps_raw, w1_ref, w2_ref))
+        ]
+
+    def z_copy(target, source):
+        return across("section", target, zst.at[target], zrec.at[source], zsend.at[target], zrecv.at[source])
+
+    def g_copy(target, source):
+        return across("section", target, gst.at[target], grec.at[source], gsend.at[target], grecv.at[source])
+
+    def part_copy(l, target, source):
+        i = lax.rem(l, blocks)
+        return across("section", target, part.at[l], arec.at[source, i], asend.at[l], arecv.at[source, i])
+
+    def restored(v16):
+        out_field[...] = packed(mm(perm_ref[...], unpacked(v16), ((0,), (0,))))
+        columns = [out_field[pl.ds(k, 16, stride=8), :] for k in range(8)]
+        return jnp.concatenate(columns, axis=1).astype(bf16)
+
+    def taken(v):
+        v = v.astype(f32)
+        for k in range(8):
+            out_field[pl.ds(k, 16, stride=8), :] = v[:, 128 * k : 128 * k + 128]
+        rows16 = unpacked(out_field[...].astype(bf16))
+        return packed(mm(perm_ref[...], rows16, ((1,), (0,))))
+
     offsets = grid_offsets(tile_count)
     north, east, south, west, ne, se, sw, nw = [
         lax.rem(me + (off % tile_count), tile_count) for off in offsets
@@ -135,16 +209,28 @@
             es[EAST, pair] = field[pl.ds(6 + pair, 16, stride=8), :]
 
     barrier = pltpu.get_barrier_semaphore()
-    partners = sorted({off % tile_count for off in offsets})
-    for off in partners:
+
+    def greet(j, carry):
         pl.semaphore_signal(
             barrier,
             inc=1,
-            device_id={"tile": lax.rem(me + off, tile_count)},
+            device_id={"tile": lax.rem(me + j, tile_count)},
             device_id_type=pl.DeviceIdType.MESH,
         )
-
-    offer(0, x_ref[...])
+        return carry
+
+    lax.fori_loop(1, tile_count, greet, 0)
+    for other in others:
+        pl.semaphore_signal(
+            barrier,
+            inc=1,
+            device_id={"section": other},
+            device_id_type=pl.DeviceIdType.MESH,
+        )
+    taps_raw[mine] = taps_own[...]
+    w1_ref[mine] = w1_own[...]
+    w2_ref[mine] = w2_own[...]
+    offer(0, taken(x_ref[mine]))
     rows = lax.broadcasted_iota(jnp.int32, (256, 128), 0)
     lanes = lax.broadcasted_iota(jnp.int32, (256, 128), 1)
     same = ((rows % 128) < 64) == (lanes < 64)
@@ -152,14 +238,28 @@
     dz[...] = jnp.zeros_like(dz)
     dodd[...] = jnp.zeros_like(dodd)
     eb[...] = jnp.zeros_like(eb)
-    pl.semaphore_wait(barrier, len(partners))
+    pl.semaphore_wait(barrier, tile_count - 1 + sections - 1)
     for copy in forward_copies(0):
         copy.start()
+    for other in others:
+        for copy in weight_copies(other, mine):
+            copy.start()
+    grad[...] = taken(ct_ref[mine])
+    total_ref[...] = jnp.zeros_like(total_ref)
+    dk_ref[...] = jnp.zeros_like(dk_ref)
 
     def low_lanes(shape):
         return lax.broadcasted_iota(jnp.int32, shape, len(shape) - 1) < 64
 
     def forward_step(l, carry):
+        sec, block = l // blocks, lax.rem(l, blocks)
+
+        @pl.when((block == 0) & (sec != mine))
+        def _():
+            for copy in weight_copies(mine, sec):
+                copy.wait_recv()
+
+        taps_ref[l] = mm(tap_perm_ref[...], taps_raw[sec, block], ((1,), (0,)))
         sent = forward_copies(l)
         for copy in sent:
             copy.wait_recv()
@@ -189,14 +289,13 @@
         inv[l] = scale
         u = unpacked(normed.astype(bf16))
         us[l] = u
-        before = mm(u, w1_ref[l], ((1,), (0,)))
+        before = mm(u, w1_ref[sec, block], ((1,), (0,)))
         t = jnp.tanh(gelu_k * (before + gelu_c * before * before * before))
         g = (0.5 * before * (1.0 + t)).astype(bf16)
         gs[l] = g
-        branch = packed(mm(g, w2_ref[l], ((1,), (0,))))
+        branch = packed(mm(g, w2_ref[sec, block], ((1,), (0,))))
         z = pad[l, 3:19, 8:16, :].reshape(128, 128) + branch
         z16 = z.astype(bf16)
-        zo_ref[l // 2] = z16
         for copy in sent:
             copy.wait_send()
 
@@ -207,6 +306,14 @@
                 copy.start()
 
         square = before * before
+        @pl.when(block == blocks - 1)
+        def _():
+            zst[sec] = restored(z16)
+
+        @pl.when((block == blocks - 1) & (sec != mine))
+        def _():
+            z_copy(sec, mine).start()
+
         slope[l] = 0.5 * (1.0 + t) + 0.5 * before * (1.0 - t * t) * gelu_k * (
             1.0 + 3.0 * gelu_c * square
         )
@@ -214,15 +321,14 @@
 
     lax.fori_loop(0, layers, forward_step, 0)
 
-    grad[...] = ct_ref[...]
-
     def backward_step(count, carry):
         l = layers - 1 - count
+        sec, block = l // blocks, lax.rem(l, blocks)
         d = grad[...]
         d_rows = unpacked(d.astype(bf16))
-        dg = mm(d_rows, w2_ref[l], ((1,), (1,)))
+        dg = mm(d_rows, w2_ref[sec, block], ((1,), (1,)))
         da = (dg * slope[l]).astype(bf16)
-        du = packed(mm(da, w1_ref[l], ((1,), (1,))))
+        du = packed(mm(da, w1_ref[sec, block], ((1,), (1,))))
         avg = averaging[...]
         normed = xhat[l]
         dh = inv[l] * (du - half_mean(du, avg) - normed * half_mean(du * normed, avg))
@@ -265,12 +371,24 @@
                     window = pad[l, a : a + 16, start : start + 8, :]
                 else:
                     window = odd[l, a : a + 16, b // 2 : b // 2 + 8, :]
-                part = jnp.sum(window * dh3, axis=0)
-                dk_ref[l, side * a + b : side * a + b + 1, :] = jnp.sum(
-                    part, axis=0, keepdims=True
+                tap_rows = jnp.sum(window * dh3, axis=0)
+                dk_ref[side * a + b : side * a + b + 1, :] = jnp.sum(
+                    tap_rows, axis=0, keepdims=True
                 )
-        dw1_ref[l] = mm(us[l], da, ((0,), (0,)))
-        dw2_ref[l] = mm(gs[l], d_rows, ((0,), (0,)))
+        grad_in = mm(us[l], da, ((0,), (0,)))
+        grad_out = mm(gs[l], d_rows, ((0,), (0,)))
+
+        part[l, 0:128] = jnp.concatenate([grad_in[:, :128], grad_in[:, 128:]], axis=0).astype(bf16)
+        part[l, 128:256] = packed(grad_out).astype(bf16)
+        tap_sums = dk_ref[...]
+        high = tap_sums.astype(bf16)
+        low = (tap_sums - high.astype(f32)).astype(bf16)
+        turn = tap_perm_ref[...]
+        part[l, 256:320] = (mm(turn, high, ((0,), (0,))) + mm(turn, low, ((0,), (0,)))).astype(bf16)
+
+        @pl.when(sec != mine)
+        def _():
+            part_copy(l, sec, mine).start()
 
         for copy in sent:
             copy.wait_recv()
@@ -286,23 +404,93 @@
                     field[pl.ds(place, 16, stride=8), :] + extra
                 )
         result = field[...].astype(bf16)
-        go_ref[l // 2] = result
         grad[...] = result.astype(f32)
+
+        @pl.when(block == 0)
+        def _():
+            gst[sec] = restored(result)
+
+        @pl.when((block == 0) & (sec != mine))
+        def _():
+            g_copy(sec, mine).start()
+
         for copy in sent:
             copy.wait_send()
         return carry
 
     lax.fori_loop(0, layers, backward_step, 0)
 
-
-def turned(n, code):
-    cells = jnp.arange(n * n, dtype=jnp.int32)
-    r, c = cells // n, cells % n
+    for i in range(blocks):
+        total = part[mine * blocks + i].astype(f32)
+        for other in others:
+            part_copy(mine * blocks + i, mine, other).wait_recv()
+            total = total + arec[other, i].astype(f32)
+        total_ref[320 * i : 320 * i + 320] = total.astype(bf16)
+
+    def place(tile):
+        return pl.ds(pl.multiple_of(tile * piece, 16), piece)
+
+    def ahead(j):
+        return lax.rem(me + j, tile_count)
+
+    def behind(j):
+        return lax.rem(me + tile_count - j, tile_count)
+
+    def scatter(j, tile):
+        return across("tile", tile, total_ref.at[place(tile)], rs.at[j], rsend.at[j], rrecv.at[j])
+
+    def spread(j, tile, source):
+        spot = place(source)
+        return across("tile", tile, fin.at[spot], fin.at[spot], csend.at[j], crecv.at[j])
+
+    def each(body):
+        def step(j, carry):
+            body(j)
+            return carry
+
+        lax.fori_loop(1, tile_count, step, 0)
+
+    each(lambda j: scatter(j, ahead(j)).start())
+
+    def gathered(j, total):
+        scatter(j, ahead(j)).wait_recv()
+        return total + rs[j].astype(f32)
+
+    total = lax.fori_loop(1, tile_count, gathered, total_ref[place(me)].astype(f32))
+    fin[place(me)] = (total * grad_scale).astype(bf16)
+    each(lambda j: spread(j, ahead(j), me).start())
+
+    zo_ref[mine] = zst[mine]
+    go_ref[mine] = gst[mine]
+    for other in others:
+        z_copy(mine, other).wait_recv()
+        zo_ref[other] = zrec[other]
+        g_copy(mine, other).wait_recv()
+        go_ref[other] = grec[other]
+    for other in others:
+        for copy in weight_copies(other, mine):
+            copy.wait_send()
+        z_copy(other, mine).wait_send()
+        g_copy(other, mine).wait_send()
+        for i in range(blocks):
+            part_copy(other * blocks + i, other, mine).wait_send()
+    each(lambda j: scatter(j, ahead(j)).wait_send())
+    each(lambda j: spread(j, me, behind(j)).wait_recv())
+    each(lambda j: spread(j, ahead(j), me).wait_send())
+    for i in range(blocks):
+        whole = fin[320 * i : 320 * i + 320].astype(f32)
+        dw1_out[i] = jnp.concatenate([whole[0:64], whole[64:128]], axis=1)
+        dw2_out[i] = unpacked(whole[128:256])
+        dk_out[i] = whole[256:305, :64] + whole[256:305, 64:]
+
+
+def turned(n, code, order):
+    r, c = order // n, order % n
     choices = [r * n + c, c * n + (n - 1 - r), (n - 1 - r) * n + (n - 1 - c), (n - 1 - c) * n + r]
     source = choices[0]
     for k in range(1, 4):
         source = jnp.where(code == k, choices[k], source)
-    return (source[:, None] == cells[None, :])
+    return (source[:, None] == order[None, :]).astype(bf16)
 
 
 def on_device(inputs, cotangent, depth_weight, in_weight, out_weight, neighbours, orientation):
@@ -312,28 +500,18 @@
     tile_count = lax.axis_size("tile")
     sections = lax.axis_size("section")
     layers = blocks * sections
-    section_id = lax.axis_index("section")
     code = orientation[lax.axis_index("tile")]
     back_code = (-code) % 4
     grad_scale = 1.0 / math.sqrt(micro_count * tile_count * extent * extent)
     pixels = extent * extent
-
-    mine = jnp.stack([inputs[:, 0], cotangent[:, 0]])
-    mine = lax.dynamic_index_in_dim(mine, section_id, 1, keepdims=False)
-    into = turned(extent, back_code).astype(bf16)
-    mine = jnp.einsum(
-        "pq,fqc->fpc", into, mine.reshape(2, pixels, channels), preferred_element_type=f32
-    )
-    mine = mine.reshape(2, pixels // 2, 2 * channels)
-
-    depth_all = lax.all_gather(depth_weight, "section", axis=0, tiled=True)
-    in_all = lax.all_gather(in_weight, "section", axis=0, tiled=True)
-    out_all = lax.all_gather(out_weight, "section", axis=0, tiled=True)
-    taps_turn = turned(side, back_code)
-    taps_all = jnp.einsum(
-        "pq,lqc->lpc", taps_turn.astype(bf16), depth_all, preferred_element_type=f32
-    )
-    taps_all = jnp.concatenate([taps_all, taps_all], axis=2)
+    piece = -(-320 * blocks // (16 * tile_count)) * 16
+
+    places = jnp.arange(pixels, dtype=jnp.int32)
+    perm = turned(extent, back_code, (places % 128) * 2 + places // 128)
+    tap_perm = turned(side, back_code, jnp.arange(taps, dtype=jnp.int32))
+    tap_perm = jnp.pad(tap_perm, ((0, 64 - taps), (0, 64 - taps)))
+    taps_own = jnp.concatenate([depth_weight, depth_weight], axis=2)
+    taps_own = jnp.pad(taps_own, ((0, 0), (0, 64 - taps), (0, 0)))
 
     ne_ok = (neighbours[0, 4 + back_code] >= 0).astype(f32)
     sw_ok = (neighbours[0, 4 + (2 - code) % 4] >= 0).astype(f32)
@@ -343,17 +521,32 @@
 
     vmem = pl.BlockSpec(memory_space=pltpu.VMEM)
     zo, go, dk, dw1, dw2 = pl.pallas_call(
-        functools.partial(kernel, tile_count, layers),
+        functools.partial(kernel, tile_count, sections, blocks, piece, grad_scale),
         out_shape=(
-            jax.ShapeDtypeStruct((sections, 128, 128), bf16),
-            jax.ShapeDtypeStruct((sections, 128, 128), bf16),
-            jax.ShapeDtypeStruct((layers, taps, 128), f32),
-            jax.ShapeDtypeStruct((layers, channels, hidden), f32),
-            jax.ShapeDtypeStruct((layers, hidden, channels), f32),
+            jax.ShapeDtypeStruct((micro_count, extent, merged), bf16),
+            jax.ShapeDtypeStruct((micro_count, extent, merged), bf16),
+            jax.ShapeDtypeStruct((blocks, taps, channels), f32),
+            jax.ShapeDtypeStruct((blocks, channels, hidden), f32),
+            jax.ShapeDtypeStruct((blocks, hidden, channels), f32),
         ),
-        in_specs=[vmem] * 6,
+        in_specs=[vmem] * 8,
         out_specs=(vmem,) * 5,
         scratch_shapes=[
+            pltpu.VMEM((sections, blocks, 64, 128), bf16),
+            pltpu.VMEM((layers, 64, 128), f32),
+            pltpu.VMEM((sections, blocks, channels, hidden), bf16),
+            pltpu.VMEM((sections, blocks, hidden, channels), bf16),
+            pltpu.VMEM((sections, 16, 1024), bf16),
+            pltpu.VMEM((sections, 16, 1024), bf16),
+            pltpu.VMEM((sections, 16, 1024), bf16),
+            pltpu.VMEM((sections, 16, 1024), bf16),
+            pltpu.VMEM((128, 128), f32),
+            pltpu.VMEM((64, 128), f32),
+            pltpu.VMEM((layers, 320, 128), bf16),
+            pltpu.VMEM((sections, blocks, 320, 128), bf16),
+            pltpu.VMEM((piece * tile_count, 128), bf16),
+            pltpu.VMEM((tile_count, piece, 128), bf16),
+            pltpu.VMEM((piece * tile_count, 128), bf16),
             pltpu.VMEM((layers, 22, 24, 128), f32),
             pltpu.VMEM((layers, 22, 16, 128), f32),
             pltpu.VMEM((2, 2, 16, 128), f32),
@@ -375,41 +568,33 @@
             pltpu.SemaphoreType.DMA((8,)),
             pltpu.SemaphoreType.DMA((layers, 8)),
             pltpu.SemaphoreType.DMA((layers, 8)),
+            pltpu.SemaphoreType.DMA((sections, 3)),
+            pltpu.SemaphoreType.DMA((sections, 3)),
+            pltpu.SemaphoreType.DMA((sections,)),
+            pltpu.SemaphoreType.DMA((sections,)),
+            pltpu.SemaphoreType.DMA((sections,)),
+            pltpu.SemaphoreType.DMA((sections,)),
+            pltpu.SemaphoreType.DMA((layers,)),
+            pltpu.SemaphoreType.DMA((sections, blocks)),
+            pltpu.SemaphoreType.DMA((tile_count,)),
+            pltpu.SemaphoreType.DMA((tile_count,)),
+            pltpu.SemaphoreType.DMA((tile_count,)),
+            pltpu.SemaphoreType.DMA((tile_count,)),
         ],
         compiler_params=pltpu.CompilerParams(
             collective_id=0, has_side_effects=True, vmem_limit_bytes=40 * 1024 * 1024
         ),
-    )(mine[0], mine[1], taps_all, in_all, out_all, mask)
-
-    fields = jnp.stack([zo, go], axis=1).reshape(sections, 2, pixels, channels)
-    outward = turned(extent, code).astype(bf16)
-    fields = jnp.einsum("pq,sfqc->sfpc", outward, fields, preferred_element_type=f32).astype(bf16)
-    fields = lax.all_to_all(fields, "section", 0, 0, tiled=True)
-    section_outputs = fields[:, 0].reshape(1, micro_count, 1, extent, merged)
-    section_grads = fields[:, 1].reshape(1, micro_count, 1, extent, merged)
-
-    dk = dk[:, :, :channels] + dk[:, :, channels:]
-    dk = jnp.einsum(
-        "pq,lqc->lpc",
-        turned(side, code).astype(f32),
-        dk,
-        precision=lax.Precision.HIGHEST,
-        preferred_element_type=f32,
+    )(
+        inputs[:, 0],
+        cotangent[:, 0],
+        taps_own,
+        in_weight,
+        out_weight,
+        mask,
+        perm,
+        tap_perm,
     )
-    sums = jnp.concatenate(
-        [dk.reshape(layers, -1), dw1.reshape(layers, -1), dw2.reshape(layers, -1)], axis=1
-    )
-    sums = lax.psum_scatter(sums, "section", scatter_dimension=0, tiled=True)
-    sums = lax.psum(sums, "tile") * grad_scale
-    cut1 = taps * channels
-    cut2 = cut1 + channels * hidden
-    return (
-        section_outputs,
-        section_grads,
-        sums[:, :cut1].reshape(blocks, taps, channels),
-        sums[:, cut1:cut2].reshape(blocks, channels, hidden),
-        sums[:, cut2:].reshape(blocks, hidden, channels),
-    )
+    return (zo[None, :, None], go[None, :, None], dk, dw1, dw2)
 
 
 def solution(mesh):

time: 267 us -> 125 us (0.47)
  waiting for transfers between devices: 100 us -> 0 us
  blocking collectives: 27.2 us -> 0 us
  Pallas kernels: 90.7 us -> 112 us
  between operations: 20.2 us -> 4.01 us
  local copies, waits for them, and re-layouts: 20.4 us -> 8.12 us
  starting transfers between devices: 3.48 us -> 0 us
    psum x1 -> x0, waiting for transfers between devices: 51.5 us -> none  [on_device(): sums = lax.psum(sums, 'tile') * grad_scale]
    unnamed x3 -> x0, waiting for transfers between devices: 48.6 us -> none
    all_gather x3 -> x0, blocking collectives: 27.2 us -> none  [the longest x1 9.92 us: on_device(): depth_all = lax.all_gather(depth_weight, 'section', axis=0, tiled=True)]
    pallas_call x1, Pallas kernels: 90.7 us -> 112 us  [on_device(): pl.pallas_call(functools.partial(kernel, tile_count, sections, blocks, pi...]
    unnamed x15 -> x21, local copies, waits for them, and re-layouts: 10.7 us -> 6.88 us
    all_to_all x1 -> x0, starting transfers between devices: 3.4 us -> none  [on_device(): fields = lax.all_to_all(fields, 'section', 0, 0, tiled=True)]
  transfers between devices with their start and end apart: 3 -> 0, of which waited for: 2 -> 0; matrix products, arithmetic and copies ran while one was open for 2% -> 0% of each run, Pallas kernels for 0% -> 0%
where the time goes in v2:
time: 125 us; the launch traced here: 124 us
  Pallas kernels  112 us (90%)
  local copies, waits for them, and re-layouts  8.12 us (6%)
  between operations  4.01 us (3%)
    pallas_call x1, Pallas kernels, on_device(): pl.pallas_call(functools.partial(kernel, tile_count, sections, blocks, pi...  112 us
    unnamed x21, local copies, waits for them, and re-layouts  6.88 us

profile of v2, /device:TPU:0, one launch (start us, length us, event | category | flops | bytes accessed | tf_op | source)
XLA Modules:
  0.0 124.2 jit_solution(3933455691539637481)
XLA Ops:
  0.6 0.0 copy-start.6
  0.6 0.6 copy-done.6
  1.3 0.6 dynamic_slice.9
  3.9 0.0 copy-start.5
  3.9 0.6 copy-done.5
  4.5 0.6 constant_dynamic-slice_fusion.1
  6.5 0.1 iota_compare_fusion.1
  6.5 0.0 copy-start.4
  6.6 0.1 broadcast_in_dim.31.mask_ref
  6.6 0.6 copy-done.4
  7.3 0.0 copy-start.3
  7.3 0.1 fusion.2.taps_own
  7.4 0.0 copy-start.1
  7.4 0.1 compare_convert_fusion.perm_ref
  7.5 0.6 copy-done.3
  8.1 0.0 copy-start
  8.1 0.0 copy-start.2
  8.1 0.1 copy.14.w2_own
  8.3 0.0 copy-done.1
  8.3 0.8 copy-done
  9.1 0.0 copy-done.2
  9.1 111.8 %shard_map.110 = (bf16[4,16,1024]{2,1,0:T(8,128)(2,1)S(1)}, bf16[4,16,1024]{2,1,0:T(8,128)(2,1)S(1)}, f32[2,49,64]{2,1,0:T(8,128)S(1)}, f32[2,64,256]{2,1,0:T(8,128)S(1)}, f32[2,256,64]{2,1,0:T(8,128)S(1)}) custom-call(bf16[4,16,1024]{2,1,0:T(8,128)(2,1)S(1)} %bitcast.13, bf16[4,16,1024]{2,1,0:T(8,128)(2,1)S(1)} %bitcast.14, ...), custom_call_target="tpu_custom_call" | custom-call | tf_op jit(solution)/shard_map/pallas_call | solution.py:523
  120.8 0.6 copy.17
  121.5 0.8 copy.18
  122.3 0.7 copy.22
  122.9 0.7 copy.23
  123.6 0.7 copy.24
  (6 shorter events, 0.1 us)
Async XLA Ops:
  0.6 0.7 copy-start.6
  3.9 0.7 copy-start.5
  6.5 0.7 copy-start.4
  7.3 0.8 copy-start.3
  7.4 0.9 copy-start.1
  8.1 0.9 copy-start
  8.1 0.9 copy-start.2

commit v3 on v2

--- a/solution.py
+++ b/solution.py
@@ -40,6 +40,14 @@
     high = v.astype(bf16)
     low = (v - high.astype(f32)).astype(bf16)
     return mm(jnp.concatenate([high, low], axis=1), averaging, ((1,), (0,)))
+
+
+def turned(n, code, place, cell):
+    r, c = place // n, place % n
+    source = place
+    for k, choice in ((1, c * n + n - 1 - r), (2, n * n - 1 - place), (3, (n - 1 - c) * n + r)):
+        source = jnp.where(code == k, choice, source)
+    return jnp.where(source == cell, 1.0, 0.0).astype(bf16)
 
 
 def kernel(
@@ -53,14 +61,17 @@
     taps_own,
     w1_own,
     w2_own,
-    mask_ref,
-    perm_ref,
-    tap_perm_ref,
+    neighbour_ref,
+    orientation_ref,
     zo_ref,
     go_ref,
     dk_out,
     dw1_out,
     dw2_out,
+    mask_ref,
+    perm_ref,
+    tap_perm_ref,
+    rims,
     taps_raw,
     taps_ref,
     w1_ref,
@@ -227,10 +238,32 @@
             device_id={"section": other},
             device_id_type=pl.DeviceIdType.MESH,
         )
-    taps_raw[mine] = taps_own[...]
+    code = orientation_ref[me]
+    back_code = lax.rem(4 - code, 4)
+    missing_ne = jnp.where(neighbour_ref[0, 4 + back_code] < 0, 1, 0)
+    missing_sw = jnp.where(neighbour_ref[0, 4 + lax.rem(6 - code, 4)] < 0, 1, 0)
+    row = lax.broadcasted_iota(jnp.int32, (22, 128), 0)
+    mask_ref[WEST] = jnp.where((row >= 19) & (missing_sw > 0), 0.0, 1.0)
+    mask_ref[EAST] = jnp.where((row < 3) & (missing_ne > 0), 0.0, 1.0)
+
+    def natural(count, axis):
+        i = lax.broadcasted_iota(jnp.int32, (count, count), axis)
+        return (i & 127) * 2 + (i >> 7)
+
+    perm_ref[...] = turned(16, back_code, natural(256, 0), natural(256, 1))
+    first = lax.broadcasted_iota(jnp.int32, (64, 64), 0)
+    second = lax.broadcasted_iota(jnp.int32, (64, 64), 1)
+    tap_turn = turned(side, back_code, first, second)
+    tap_perm_ref[...] = jnp.where((first < 49) & (second < 49), tap_turn, jnp.zeros_like(tap_turn))
+    dk_ref[...] = jnp.zeros_like(dk_ref)
+    for i in range(blocks):
+        own = taps_own[i].astype(f32)
+        dk_ref[0:49, :] = jnp.concatenate([own, own], axis=1)
+        taps_raw[mine, i] = dk_ref[...].astype(bf16)
     w1_ref[mine] = w1_own[...]
     w2_ref[mine] = w2_own[...]
-    offer(0, taken(x_ref[mine]))
+    offer(0, taken(x_ref[mine, 0]))
+    rims[...] = jnp.zeros_like(rims)
     rows = lax.broadcasted_iota(jnp.int32, (256, 128), 0)
     lanes = lax.broadcasted_iota(jnp.int32, (256, 128), 1)
     same = ((rows % 128) < 64) == (lanes < 64)
@@ -244,9 +277,8 @@
     for other in others:
         for copy in weight_copies(other, mine):
             copy.start()
-    grad[...] = taken(ct_ref[mine])
+    grad[...] = taken(ct_ref[mine, 0])
     total_ref[...] = jnp.zeros_like(total_ref)
-    dk_ref[...] = jnp.zeros_like(dk_ref)
 
     def low_lanes(shape):
         return lax.broadcasted_iota(jnp.int32, shape, len(shape) - 1) < 64
@@ -341,28 +373,49 @@
             )
             rolled = pltpu.roll(merged.reshape(128, 128), 64, 1).reshape(16, 8, 128)
             dodd[6:22, start : start + 8, :] = rolled
-        for top in (0, 11):
-            total = jnp.zeros((11, 16, 128), f32)
-            for a in range(side):
-                for b in range(side):
-                    shift = 3 - b
-                    first = top + 6 - a
-                    if shift % 2 == 0:
-                        start = 6 + shift // 2
-                        window = dz[first : first + 11, start : start + 16, :]
-                    else:
-                        start = 6 + (shift - 1) // 2
-                        window = dodd[first : first + 11, start : start + 16, :]
-                    total = total + window * taps_ref[l, side * a + b]
-            dp[top : top + 11, 6:22, :] = total
+        for top in (0, 19):
+            total = [jnp.zeros((16, 128), f32) for _ in range(3)]
+            for b in range(side):
+                shift = 3 - b
+                ref = dodd if shift % 2 else dz
+                start = 6 + shift // 2
+                for q in range(3):
+                    for a in range(side):
+                        if not 0 <= top + q - a <= 15:
+                            continue
+                        window = ref[top + q + 6 - a, start : start + 16, :]
+                        total[q] = total[q] + window * taps_ref[l, side * a + b]
+            for q in range(3):
+                dp[top + q, 6:22, :] = total[q]
+        sources = (((dz, 8), (dodd, 7), (dodd, 8)), ((dz, 15), (dodd, 15), (dodd, 14)))
         for edge in range(2):
+            for k, (ref, pair) in enumerate(sources[edge]):
+                rims[edge, k, 6:22, :] = ref[6:22, pair : pair + 1, :].reshape(16, 128)
+        uses = (
+            ((0, 0, 1), (1, 0, 2), (1, 1, 0), (1, 2, 1)),
+            ((0, 4, 1), (0, 5, 0), (0, 6, 2), (1, 6, 1)),
+        )
+        for edge in range(2):
+            total = [jnp.zeros((22, 128), f32) for _ in range(2)]
+            for pair, b, k in uses[edge]:
+                for a in range(side):
+                    window = rims[edge, k, 6 - a : 28 - a, :]
+                    total[pair] = total[pair] + window * taps_ref[l, side * a + b]
             for pair in range(2):
-                place = (6 if edge == WEST else 16) + pair
-                column = dp[:, place : place + 1, :].reshape(22, 128)
-                eb[edge, pair, 5:27, :] = column * mask_ref[edge]
+                eb[edge, pair, 5:27, :] = total[pair] * mask_ref[edge]
         sent = backward_copies(l)
         for copy in sent:
             copy.start()
+
+        centre = jnp.zeros((16, 8, 128), f32)
+        for a in range(side):
+            for b in range(side):
+                shift = 3 - b
+                ref = dodd if shift % 2 else dz
+                start = 8 + shift // 2
+                window = ref[9 - a : 25 - a, start : start + 8, :]
+                centre = centre + window * taps_ref[l, side * a + b]
+        grad[...] = d + centre.reshape(128, 128)
 
         for a in range(side):
             for b in range(side):
@@ -392,7 +445,7 @@
 
         for copy in sent:
             copy.wait_recv()
-        base = d.reshape(16, 8, 128) + dp[3:19, 8:16, :]
+        base = grad[...].reshape(16, 8, 128)
         top_part = base[0:3] + bn[l, 0]
         bottom_part = base[13:16] + bn[l, 1]
         field[...] = jnp.concatenate([top_part, base[3:13], bottom_part], axis=0).reshape(128, 128)
@@ -460,13 +513,13 @@
     fin[place(me)] = (total * grad_scale).astype(bf16)
     each(lambda j: spread(j, ahead(j), me).start())
 
-    zo_ref[mine] = zst[mine]
-    go_ref[mine] = gst[mine]
+    zo_ref[0, mine, 0] = zst[mine]
+    go_ref[0, mine, 0] = gst[mine]
     for other in others:
         z_copy(mine, other).wait_recv()
-        zo_ref[other] = zrec[other]
+        zo_ref[0, other, 0] = zrec[other]
         g_copy(mine, other).wait_recv()
-        go_ref[other] = grec[other]
+        go_ref[0, other, 0] = grec[other]
     for other in others:
         for copy in weight_copies(other, mine):
             copy.wait_send()
@@ -484,15 +537,6 @@
         dk_out[i] = whole[256:305, :64] + whole[256:305, 64:]
 
 
-def turned(n, code, order):
-    r, c = order // n, order % n
-    choices = [r * n + c, c * n + (n - 1 - r), (n - 1 - r) * n + (n - 1 - c), (n - 1 - c) * n + r]
-    source = choices[0]
-    for k in range(1, 4):
-        source = jnp.where(code == k, choices[k], source)
-    return (source[:, None] == order[None, :]).astype(bf16)
-
-
 def on_device(inputs, cotangent, depth_weight, in_weight, out_weight, neighbours, orientation):
     micro_count, _, extent, merged = inputs.shape
     blocks, taps, channels = depth_weight.shape
@@ -500,38 +544,27 @@
     tile_count = lax.axis_size("tile")
     sections = lax.axis_size("section")
     layers = blocks * sections
-    code = orientation[lax.axis_index("tile")]
-    back_code = (-code) % 4
     grad_scale = 1.0 / math.sqrt(micro_count * tile_count * extent * extent)
-    pixels = extent * extent
     piece = -(-320 * blocks // (16 * tile_count)) * 16
 
-    places = jnp.arange(pixels, dtype=jnp.int32)
-    perm = turned(extent, back_code, (places % 128) * 2 + places // 128)
-    tap_perm = turned(side, back_code, jnp.arange(taps, dtype=jnp.int32))
-    tap_perm = jnp.pad(tap_perm, ((0, 64 - taps), (0, 64 - taps)))
-    taps_own = jnp.concatenate([depth_weight, depth_weight], axis=2)
-    taps_own = jnp.pad(taps_own, ((0, 0), (0, 64 - taps), (0, 0)))
-
-    ne_ok = (neighbours[0, 4 + back_code] >= 0).astype(f32)
-    sw_ok = (neighbours[0, 4 + (2 - code) % 4] >= 0).astype(f32)
-    rows = jnp.arange(extent + 2 * rim)
-    mask = jnp.stack([jnp.where(rows >= 19, sw_ok, 1.0), jnp.where(rows < 3, ne_ok, 1.0)])
-    mask = jnp.broadcast_to(mask[:, :, None], (2, extent + 2 * rim, 128))
-
     vmem = pl.BlockSpec(memory_space=pltpu.VMEM)
+    smem = pl.BlockSpec(memory_space=pltpu.SMEM)
     zo, go, dk, dw1, dw2 = pl.pallas_call(
         functools.partial(kernel, tile_count, sections, blocks, piece, grad_scale),
         out_shape=(
-            jax.ShapeDtypeStruct((micro_count, extent, merged), bf16),
-            jax.ShapeDtypeStruct((micro_count, extent, merged), bf16),
+            jax.ShapeDtypeStruct((1, micro_count, 1, extent, merged), bf16),
+            jax.ShapeDtypeStruct((1, micro_count, 1, extent, merged), bf16),
             jax.ShapeDtypeStruct((blocks, taps, channels), f32),
             jax.ShapeDtypeStruct((blocks, channels, hidden), f32),
             jax.ShapeDtypeStruct((blocks, hidden, channels), f32),
         ),
-        in_specs=[vmem] * 8,
+        in_specs=[vmem] * 5 + [smem] * 2,
         out_specs=(vmem,) * 5,
         scratch_shapes=[
+            pltpu.VMEM((2, 22, 128), f32),
+            pltpu.VMEM((256, 256), bf16),
+            pltpu.VMEM((64, 64), bf16),
+            pltpu.VMEM((2, 3, 32, 128), f32),
             pltpu.VMEM((sections, blocks, 64, 128), bf16),
             pltpu.VMEM((layers, 64, 128), f32),
             pltpu.VMEM((sections, blocks, channels, hidden), bf16),
@@ -584,17 +617,8 @@
         compiler_params=pltpu.CompilerParams(
             collective_id=0, has_side_effects=True, vmem_limit_bytes=40 * 1024 * 1024
         ),
-    )(
-        inputs[:, 0],
-        cotangent[:, 0],
-        taps_own,
-        in_weight,
-        out_weight,
-        mask,
-        perm,
-        tap_perm,
-    )
-    return (zo[None, :, None], go[None, :, None], dk, dw1, dw2)
+    )(inputs, cotangent, depth_weight, in_weight, out_weight, neighbours, orientation)
+    return (zo, go, dk, dw1, dw2)
 
 
 def solution(mesh):

time: 125 us -> 115 us (0.920)
  Pallas kernels: 112 us -> 108 us
  between operations: 4.01 us -> 0.71 us
  local copies, waits for them, and re-layouts: 8.12 us -> 6.08 us
    pallas_call x1, Pallas kernels: 112 us -> 108 us  [on_device(): pl.pallas_call(functools.partial(kernel, tile_count, sections, blocks, pi...]
    unnamed x21 -> x15, local copies, waits for them, and re-layouts: 6.88 us -> 4.66 us
    pallas_call x0 -> x2, local copies, waits for them, and re-layouts: none -> 1.42 us  [on_device(): pl.pallas_call(functools.partial(kernel, tile_count, sections, blocks, pi...]
where the time goes in v3:
time: 115 us
  Pallas kernels  108 us (94%)
  local copies, waits for them, and re-layouts  6.08 us (5%)
    pallas_call x1, Pallas kernels, on_device(): pl.pallas_call(functools.partial(kernel, tile_count, sections, blocks, pi...  108 us
    unnamed x15, local copies, waits for them, and re-layouts  4.66 us

profile of v3, /device:TPU:0, one launch (start us, length us, event | category | flops | bytes accessed | tf_op | source)
XLA Modules:
  0.0 114.5 jit_solution(7045786346365208458)
XLA Ops:
  0.6 0.0 copy-start
  0.6 0.8 copy.12.taps_own
  1.4 0.0 copy-start.2
  1.4 0.0 copy-start.3
  1.4 0.0 copy-start.4
  1.4 1.0 copy.13.w2_own
  2.4 0.0 copy-done
  2.5 0.0 copy-done.2
  2.5 0.0 copy-done.3
  2.5 0.0 copy-done.4
  2.5 0.0 copy-start.1
  2.5 0.9 copy-done.1
  3.4 107.7 %shard_map.110 = (bf16[1,4,1,16,1024]{4,3,2,1,0:T(8,128)(2,1)S(1)}, bf16[1,4,1,16,1024]{4,3,2,1,0:T(8,128)(2,1)S(1)}, f32[2,49,64]{2,1,0:T(8,128)S(1)}, f32[2,64,256]{2,1,0:T(8,128)S(1)}, f32[2,256,64]{2,1,0:T(8,128)S(1)}) custom-call(bf16[4,1,16,1024]{3,2,1,0:T(8,128)(2,1)S(1)} %copy-done, bf16[4,1,16,1024]{3,2,1,0:T(8,128)(2,1)S(1)} %copy-done.1, ...), custom_call_target="tpu_custom_call" | custom-call | tf_op jit(solution)/shard_map/pallas_call | solution.py:552
  111.1 0.6 copy.14
  111.8 0.8 copy.15
  112.6 0.7 copy.19
  113.2 0.7 copy.20
  113.9 0.7 copy.21
Async XLA Ops:
  0.6 1.8 %copy-start = (bf16[4,1,16,1024]{3,2,1,0:T(8,128)(2,1)S(1)}, bf16[4,1,16,1024]{3,2,1,0:T(8,128)(2,1)}, u32[]{:S(2)}) copy-start(bf16[4,1,16,1024]{3,2,1,0:T(8,128)(2,1)} %x_ref.1) | copy-start | bytes 393220
  1.4 1.0 copy-start.2
  1.4 1.0 copy-start.3
  1.4 1.1 copy-start.4
  2.5 0.9 copy-start.1

commit v4 on v3

--- a/solution.py
+++ b/solution.py
@@ -89,7 +89,12 @@
     fin,
     pad,
     odd,
-    es,
+    rows_out,
+    edge_out,
+    corner_out,
+    rows_in,
+    edge_in,
+    corner_in,
     fr,
     xhat,
     inv,
@@ -100,8 +105,6 @@
     dodd,
     dp,
     eb,
-    br,
-    bn,
     field,
     grad,
     averaging,
@@ -182,42 +185,42 @@
             for i, (target, src, dst) in enumerate(plan)
         ]
 
-    def forward_copies(l):
+    def halo_copies(slot, recv):
         return copies(
             [
-                (north, pad.at[l, 3:6, 8:16], pad.at[l, 19:22, 8:16]),
-                (south, pad.at[l, 16:19, 8:16], pad.at[l, 0:3, 8:16]),
-                (nw, es.at[WEST, :, 0:8], fr.at[l, EAST, :, 24:32]),
-                (ne, es.at[EAST, :, 0:8], fr.at[l, WEST, :, 24:32]),
-                (se, es.at[EAST, :, 8:16], fr.at[l, WEST, :, 0:8]),
-                (sw, es.at[WEST, :, 8:16], fr.at[l, EAST, :, 0:8]),
-                (east, es.at[EAST], fr.at[l, WEST, :, 8:24]),
-                (west, es.at[WEST], fr.at[l, EAST, :, 8:24]),
+                (north, rows_out.at[0], rows_in.at[slot, 1]),
+                (south, rows_out.at[1], rows_in.at[slot, 0]),
+                (nw, corner_out.at[WEST, 0], corner_in.at[slot, EAST, 1]),
+                (ne, corner_out.at[EAST, 0], corner_in.at[slot, WEST, 1]),
+                (se, corner_out.at[EAST, 1], corner_in.at[slot, WEST, 0]),
+                (sw, corner_out.at[WEST, 1], corner_in.at[slot, EAST, 0]),
+                (east, edge_out.at[EAST], edge_in.at[slot, WEST]),
+                (west, edge_out.at[WEST], edge_in.at[slot, EAST]),
             ],
-            frecv.at[l],
+            recv,
         )
 
+    def forward_copies(l):
+        return halo_copies(l, frecv.at[l])
+
     def backward_copies(l):
-        return copies(
-            [
-                (north, dp.at[0:3, 8:16], bn.at[l, 1]),
-                (south, dp.at[19:22, 8:16], bn.at[l, 0]),
-                (nw, eb.at[WEST, :, 0:8], br.at[l, EAST, :, 24:32]),
-                (ne, eb.at[EAST, :, 0:8], br.at[l, WEST, :, 24:32]),
-                (se, eb.at[EAST, :, 24:32], br.at[l, WEST, :, 16:24]),
-                (sw, eb.at[WEST, :, 24:32], br.at[l, EAST, :, 16:24]),
-                (east, eb.at[EAST, :, 8:24], br.at[l, WEST, :, 0:16]),
-                (west, eb.at[WEST, :, 8:24], br.at[l, EAST, :, 0:16]),
-            ],
-            brecv.at[l],
-        )
+        return halo_copies(layers + l, brecv.at[l])
+
+    def joined(*parts):
+        return jnp.concatenate(parts, axis=0).astype(bf16)
 
     def offer(l, z):
-        pad[l, 3:19, 8:16, :] = z.reshape(16, 8, 128)
+        z3 = z.reshape(16, 8, 128)
+        pad[l, 3:19, 8:16, :] = z3
         field[...] = z
-        for pair in range(2):
-            es[WEST, pair] = field[pl.ds(pair, 16, stride=8), :]
-            es[EAST, pair] = field[pl.ds(6 + pair, 16, stride=8), :]
+        rows_out[0] = z[0:32].astype(bf16)
+        rows_out[1] = z[96:128].astype(bf16)
+        for edge, base in ((WEST, 0), (EAST, 6)):
+            one = field[pl.ds(base, 16, stride=8), :]
+            two = field[pl.ds(base + 1, 16, stride=8), :]
+            edge_out[edge] = joined(one, two)
+            corner_out[edge, 0] = joined(one[0:8], two[0:8])
+            corner_out[edge, 1] = joined(one[8:16], two[8:16])
 
     barrier = pltpu.get_barrier_semaphore()
 
@@ -271,6 +274,7 @@
     dz[...] = jnp.zeros_like(dz)
     dodd[...] = jnp.zeros_like(dodd)
     eb[...] = jnp.zeros_like(eb)
+    dp[...] = jnp.zeros_like(dp)
     pl.semaphore_wait(barrier, tile_count - 1 + sections - 1)
     for copy in forward_copies(0):
         copy.start()
@@ -295,9 +299,17 @@
         sent = forward_copies(l)
         for copy in sent:
             copy.wait_recv()
+        pad[l, 0:3, 8:16, :] = rows_in[l, 0].astype(f32).reshape(4, 8, 128)[1:4]
+        pad[l, 19:22, 8:16, :] = rows_in[l, 1].astype(f32).reshape(4, 8, 128)[0:3]
         for edge in range(2):
+            sides = edge_in[l, edge].astype(f32)
+            upper = corner_in[l, edge, 0].astype(f32)
+            lower = corner_in[l, edge, 1].astype(f32)
             for pair in range(2):
-                column = fr[l, edge, pair, 5:27, :] * mask_ref[edge]
+                fr[edge, pair, 0:8] = upper[8 * pair : 8 * pair + 8]
+                fr[edge, pair, 8:24] = sides[16 * pair : 16 * pair + 16]
+                fr[edge, pair, 24:32] = lower[8 * pair : 8 * pair + 8]
+                column = fr[edge, pair, 5:27, :] * mask_ref[edge]
                 place = (6 if edge == WEST else 16) + pair
                 pad[l, :, place : place + 1, :] = column.reshape(22, 1, 128)
         keep = low_lanes((22, 16, 128))
@@ -403,6 +415,12 @@
                     total[pair] = total[pair] + window * taps_ref[l, side * a + b]
             for pair in range(2):
                 eb[edge, pair, 5:27, :] = total[pair] * mask_ref[edge]
+        rows_out[0] = dp[0:4, 8:16, :].reshape(32, 128).astype(bf16)
+        rows_out[1] = dp[18:22, 8:16, :].reshape(32, 128).astype(bf16)
+        for edge in range(2):
+            edge_out[edge] = joined(eb[edge, 0, 8:24], eb[edge, 1, 8:24])
+            corner_out[edge, 0] = joined(eb[edge, 0, 0:8], eb[edge, 1, 0:8])
+            corner_out[edge, 1] = joined(eb[edge, 0, 24:32], eb[edge, 1, 24:32])
         sent = backward_copies(l)
         for copy in sent:
             copy.start()
@@ -446,13 +464,18 @@
         for copy in sent:
             copy.wait_recv()
         base = grad[...].reshape(16, 8, 128)
-        top_part = base[0:3] + bn[l, 0]
-        bottom_part = base[13:16] + bn[l, 1]
+        slot = layers + l
+        top_part = base[0:3] + rows_in[slot, 0].astype(f32).reshape(4, 8, 128)[1:4]
+        bottom_part = base[13:16] + rows_in[slot, 1].astype(f32).reshape(4, 8, 128)[0:3]
         field[...] = jnp.concatenate([top_part, base[3:13], bottom_part], axis=0).reshape(128, 128)
         for edge in range(2):
+            sides = edge_in[slot, edge].astype(f32)
+            upper = corner_in[slot, edge, 0].astype(f32)
+            lower = corner_in[slot, edge, 1].astype(f32)
             for pair in range(2):
                 place = (0 if edge == WEST else 6) + pair
-                extra = br[l, edge, pair, 0:16, :] + br[l, edge, pair, 16:32, :]
+                corners = [upper[8 * pair : 8 * pair + 8], lower[8 * pair : 8 * pair + 8]]
+                extra = sides[16 * pair : 16 * pair + 16] + jnp.concatenate(corners, axis=0)
                 field[pl.ds(place, 16, stride=8), :] = (
                     field[pl.ds(place, 16, stride=8), :] + extra
                 )
@@ -582,8 +605,13 @@
             pltpu.VMEM((piece * tile_count, 128), bf16),
             pltpu.VMEM((layers, 22, 24, 128), f32),
             pltpu.VMEM((layers, 22, 16, 128), f32),
-            pltpu.VMEM((2, 2, 16, 128), f32),
-            pltpu.VMEM((layers, 2, 2, 32, 128), f32),
+            pltpu.VMEM((2, 32, 128), bf16),
+            pltpu.VMEM((2, 32, 128), bf16),
+            pltpu.VMEM((2, 2, 16, 128), bf16),
+            pltpu.VMEM((2 * layers, 2, 32, 128), bf16),
+            pltpu.VMEM((2 * layers, 2, 32, 128), bf16),
+            pltpu.VMEM((2 * layers, 2, 2, 16, 128), bf16),
+            pltpu.VMEM((2, 2, 32, 128), f32),
             pltpu.VMEM((layers, 128, 128), f32),
             pltpu.VMEM((layers, 128, 128), f32),
             pltpu.VMEM((layers, 256, 64), bf16),
@@ -593,8 +621,6 @@
             pltpu.VMEM((28, 24, 128), f32),
             pltpu.VMEM((22, 24, 128), f32),
             pltpu.VMEM((2, 2, 32, 128), f32),
-            pltpu.VMEM((layers, 2, 2, 32, 128), f32),
-            pltpu.VMEM((layers, 2, 3, 8, 128), f32),
             pltpu.VMEM((128, 128), f32),
             pltpu.VMEM((128, 128), f32),
             pltpu.VMEM((256, 128), bf16),

time: 115 us -> 108 us (0.939)
  Pallas kernels: 108 us -> 101 us
    pallas_call x1, Pallas kernels: 108 us -> 101 us  [on_device(): pl.pallas_call(functools.partial(kernel, tile_count, sections, blocks, pi...]
where the time goes in v4:
time: 108 us
  Pallas kernels  101 us (94%)
  local copies, waits for them, and re-layouts  6.08 us (6%)
    pallas_call x1, Pallas kernels, on_device(): pl.pallas_call(functools.partial(kernel, tile_count, sections, blocks, pi...  101 us
    unnamed x15, local copies, waits for them, and re-layouts  4.66 us

profile of v4, /device:TPU:0, one launch (start us, length us, event | category | flops | bytes accessed | tf_op | source)
XLA Modules:
  0.0 108.1 jit_solution(17259228055249493401)
XLA Ops:
  0.6 0.0 copy-start
  0.6 0.8 copy.12.taps_own
  1.4 0.0 copy-start.2
  1.4 0.0 copy-start.3
  1.4 0.0 copy-start.4
  1.4 1.0 copy.13.w2_own
  2.4 0.0 copy-done
  2.5 0.0 copy-done.2
  2.5 0.0 copy-done.3
  2.5 0.0 copy-done.4
  2.5 0.0 copy-start.1
  2.5 0.9 copy-done.1
  3.4 101.3 %shard_map.110 = (bf16[1,4,1,16,1024]{4,3,2,1,0:T(8,128)(2,1)S(1)}, bf16[1,4,1,16,1024]{4,3,2,1,0:T(8,128)(2,1)S(1)}, f32[2,49,64]{2,1,0:T(8,128)S(1)}, f32[2,64,256]{2,1,0:T(8,128)S(1)}, f32[2,256,64]{2,1,0:T(8,128)S(1)}) custom-call(bf16[4,1,16,1024]{3,2,1,0:T(8,128)(2,1)S(1)} %copy-done, bf16[4,1,16,1024]{3,2,1,0:T(8,128)(2,1)S(1)} %copy-done.1, ...), custom_call_target="tpu_custom_call" | custom-call | tf_op jit(solution)/shard_map/pallas_call | solution.py:575
  104.7 0.6 copy.14
  105.3 0.8 copy.15
  106.1 0.7 copy.19
  106.8 0.7 copy.20
  107.4 0.7 copy.21
Async XLA Ops:
  0.6 1.8 %copy-start = (bf16[4,1,16,1024]{3,2,1,0:T(8,128)(2,1)S(1)}, bf16[4,1,16,1024]{3,2,1,0:T(8,128)(2,1)}, u32[]{:S(2)}) copy-start(bf16[4,1,16,1024]{3,2,1,0:T(8,128)(2,1)} %x_ref.1) | copy-start | bytes 393220
  1.4 1.0 copy-start.2
  1.4 1.0 copy-start.3
  1.4 1.1 copy-start.4
  2.5 0.9 copy-start.1
